TPU v7x, 512 devices: a whole 4x4x16 slice. The times are simulated.
512 devices in a mesh: row: 32 (over x_lo, z), col: 16 (over x_hi, y, core).
Axes of the slice: x: 4 (x_hi: 2, x_lo: 2; x = x_hi * 2 + x_lo), y: 4, z: 16, core: 2. Of those that a mesh axis runs over, the one named last changes fastest.
Arguments:
- a_blocks: bfloat16 [32, 16, 80, 128, 128], P('row', 'col'), may hold values from -6 to 6
- a_rows: int32 [32, 16, 80], P('row', 'col'), may hold values from 0 to 7, as said below
- a_cols: int32 [32, 16, 80], P('row', 'col'), may hold values from 0 to 15, as said below
- a_count: int32 [32, 16], P('row', 'col'), may hold values from 27 to 80, as said below
- b_blocks: bfloat16 [32, 16, 20, 128, 128], P('row', 'col'), may hold values from -0.125 to 0.125
- b_rows: int32 [32, 16, 20], P('row', 'col'), may hold values from 0 to 15, as said below
- b_cols: int32 [32, 16, 20], P('row', 'col'), may hold values from 0 to 1, as said below
- b_count: int32 [32, 16], P('row', 'col'), may hold values from 7 to 20, as said below
Outputs:
- c_slab: bfloat16 [32768, 4096], P('row', 'col')
Inputs may be any that keep to these rules, and one draw needn't show every extreme that they name: `a_rows`: within one panel the live slots name distinct blocks; slots at or past the count hold blocks that are not used, with indices in range. `a_cols`: paired slot by slot with a_rows. `a_count`: some panel is full in every draw. `b_rows`: within one panel the live slots name distinct blocks; slots at or past the count hold blocks that are not used, with indices in range. `b_cols`: paired slot by slot with b_rows. `b_count`: some panel is full in every draw.
All inputs are finite; a program needn't handle non-finite values.
Results may differ from a plain program's by a relative error of at most 0.001.
Values may be sent and summed in bfloat16 or wider, within the bound.
A program may use at most 128 MiB of HBM per device.

v0:
```python
import jax
import jax.numpy as jnp
from jax import lax
from jax.sharding import PartitionSpec as P

RB = 8
KB = 16
CB = 2
STEPS = 4


def passed_along(block, axis, distance):
    devices = range(lax.axis_size(axis))
    route = [((i - distance) % len(devices), i) for i in devices]
    return lax.ppermute(block, axis, route)


def slot_tables(rows, cols, count, block_rows, block_cols):
    slots = jnp.arange(rows.shape[0], dtype=jnp.int32)
    live = (slots < count).astype(jnp.float32)
    row_hot = (rows[:, None] == jnp.arange(block_rows, dtype=jnp.int32)[None, :]).astype(
        jnp.float32
    ) * live[:, None]
    col_hot = (cols[:, None] == jnp.arange(block_cols, dtype=jnp.int32)[None, :]).astype(
        jnp.float32
    )
    return (row_hot, col_hot)


def densify(blocks, rows, cols, count, block_rows, block_cols):
    row_hot, col_hot = slot_tables(rows, cols, count, block_rows, block_cols)
    slot_count = blocks.shape[0]
    size = blocks.shape[1]
    pair_hot = (row_hot[:, :, None] * col_hot[:, None, :]).reshape(
        slot_count, block_rows * block_cols
    )
    placed = jnp.dot(
        pair_hot.astype(jnp.bfloat16).T,
        blocks.reshape(slot_count, size * size),
        preferred_element_type=jnp.float32,
    )
    placed = placed.reshape(block_rows, block_cols, size, size).transpose(0, 2, 1, 3)
    return placed.reshape(block_rows * size, block_cols * size).astype(jnp.bfloat16)


def panel_product(a_cargo, b_cargo):
    a_blocks, a_rows, a_cols, a_count = a_cargo
    b_blocks, b_rows, b_cols, b_count = b_cargo
    b_dense = densify(b_blocks, b_rows, b_cols, b_count, KB, CB)
    a_dense = densify(a_blocks, a_rows, a_cols, a_count, RB, KB)
    return jnp.dot(a_dense, b_dense, preferred_element_type=jnp.float32)


def per_device(a_blocks, a_rows, a_cols, a_count, b_blocks, b_rows, b_cols, b_count):
    a_first = (a_blocks[0, 0], a_rows[0, 0], a_cols[0, 0], a_count[0, 0])
    b_first = (b_blocks[0, 0], b_rows[0, 0], b_cols[0, 0], b_count[0, 0])
    a_held = a_first
    b_held = b_first
    total = panel_product(a_first, b_first)
    for shift_step in range(1, STEPS):
        a_held = passed_along((a_held[0], a_held[1], a_held[2], a_held[3]), "col", -1)
        b_held = passed_along((b_held[0], b_held[1], b_held[2], b_held[3]), "row", -1)
        total = total + panel_product(a_held, b_held)
    return total.astype(jnp.bfloat16)


def solution(mesh):
    placed = (
        P("row", "col", None, None, None),
        P("row", "col", None),
        P("row", "col", None),
        P("row", "col"),
        P("row", "col", None, None, None),
        P("row", "col", None),
        P("row", "col", None),
        P("row", "col"),
    )
    return jax.shard_map(
        per_device, mesh=mesh, in_specs=placed, out_specs=P("row", "col"), check_vma=False
    )
```

profile of v0, /device:TPU:25, one launch (start us, length us, event | category | flops | bytes accessed | tf_op | source)
XLA Modules:
  0.0 241.5 jit_solution(9526578663639120319)
XLA Ops:
  0.0 12.0 %collective-permute-start.4 = (s32[20]{0:T(128)}, s32[20]{0:T(128)S(1)}, u32[]{:S(2)}, u32[]{:S(2)}) collective-permute-start(s32[20]{0:T(128)} %bitcast.292), channel_id=1, source_target_pairs={{16,0},{32,16},{48,32},{64,48},{80,64},{96,80},{112,96},{128,112},... | collective-permute-start | bytes 248 | tf_op jit(solution)/shard_map/ppermute | solution.py:15
  12.0 2.6 %collective-permute-start.5 = (s32[]{:T(128)}, s32[]{:T(128)}, u32[]{:S(2)}, u32[]{:S(2)}) collective-permute-start(s32[]{:T(128)} %bitcast.12), channel_id=1, source_target_pairs={{16,0},{32,16},{48,32},{64,48},{80,64},{96,80},{112,96},{128,112},... | collective-permute-start | bytes 20 | tf_op jit(solution)/shard_map/ppermute | solution.py:15
  14.7 2.6 %collective-permute-start.6 = (s32[20]{0:T(128)}, s32[20]{0:T(128)S(1)}, u32[]{:S(2)}, u32[]{:S(2)}) collective-permute-start(s32[20]{0:T(128)} %bitcast.298), channel_id=1, source_target_pairs={{16,0},{32,16},{48,32},{64,48},{80,64},{96,80},{112,96},{128,112},... | collective-permute-start | bytes 248 | tf_op jit(solution)/shard_map/ppermute | solution.py:15
  17.3 2.6 %collective-permute-start.7 = (bf16[20,128,128]{2,1,0:T(8,128)(2,1)}, bf16[20,128,128]{2,1,0:T(8,128)(2,1)S(1)}, u32[]{:S(2)}, u32[]{:S(2)}) collective-permute-start(bf16[20,128,128]{2,1,0:T(8,128)(2,1)} %bitcast.290), channel_id=1, source_target_pairs={{16,0},{32,16},{48,32},{64,48},{80,64},{96,80},{112,96},{128,112},... | collective-permute-start | bytes 1966088 | tf_op jit(solution)/shard_map/ppermute | solution.py:15
  20.0 3.7 %collective-permute-start.3 = (bf16[80,128,128]{2,1,0:T(8,128)(2,1)}, bf16[80,128,128]{2,1,0:T(8,128)(2,1)}, u32[]{:S(2)}, u32[]{:S(2)}) collective-permute-start(bf16[80,128,128]{2,1,0:T(8,128)(2,1)} %bitcast.284), channel_id=1, source_target_pairs={{1,0},{2,1},{3,2},{4,3},{5,4},{6,5},{7,6},{8,7},{9,8},{10,9},{11,1... | collective-permute-start | bytes 7864328 | tf_op jit(solution)/shard_map/ppermute | solution.py:15
  29.8 6.2 %convolution_convert_fusion.3 = bf16[8,16,128,128]{3,1,2,0:T(8,128)(2,1)} fusion(f32[80,16]{0,1:T(8,128)S(1)} %fusion.72, f32[80,8]{0,1:T(8,128)S(1)} %fusion.80, bf16[10,8,128,128]{3,2,1,0:T(8,128)(2,1)} %bitcast.285), kind=kOutput, calls=%fused_computation.15 | convolution fusion | flops 337661952 | bytes 6823424 | tf_op jit(solution)/shard_map/dot_general | solution.py:37
  35.9 1.9 collective-permute-start.1
  38.6 18.3 %collective-permute-done.1 = s32[]{:T(128)} collective-permute-done((s32[]{:T(128)}, s32[]{:T(128)}, u32[]{:S(2)}, u32[]{:S(2)}) %collective-permute-start.1) | collective-permute-done | bytes 36 | tf_op jit(solution)/shard_map/ppermute | solution.py:15
  56.9 12.5 %collective-permute-start.13 = (s32[]{:T(128)}, s32[]{:T(128)}, u32[]{:S(2)}, u32[]{:S(2)}) collective-permute-start(s32[]{:T(128)} %collective-permute-done.5), channel_id=1, source_target_pairs={{16,0},{32,16},{48,32},{64,48},{80,64},{96,80},{112,96},{128,112},... | collective-permute-start | bytes 20 | tf_op jit(solution)/shard_map/ppermute | solution.py:15
  72.9 6.2 %collective-permute-done.9 = s32[]{:T(128)} collective-permute-done((s32[]{:T(128)}, s32[]{:T(128)}, u32[]{:S(2)}, u32[]{:S(2)}) %collective-permute-start.9) | collective-permute-done | bytes 36 | tf_op jit(solution)/shard_map/ppermute | solution.py:15
  79.1 5.6 %collective-permute-start.21 = (s32[]{:T(128)}, s32[]{:T(128)}, u32[]{:S(2)}, u32[]{:S(2)}) collective-permute-start(s32[]{:T(128)} %collective-permute-done.13), channel_id=1, source_target_pairs={{16,0},{32,16},{48,32},{64,48},{80,64},{96,80},{112,96},{128,112},... | collective-permute-start | bytes 20 | tf_op jit(solution)/shard_map/ppermute | solution.py:15
  88.0 6.0 %collective-permute-done.17 = s32[]{:T(128)} collective-permute-done((s32[]{:T(128)}, s32[]{:T(128)}, u32[]{:S(2)}, u32[]{:S(2)}) %collective-permute-start.17) | collective-permute-done | bytes 36 | tf_op jit(solution)/shard_map/ppermute | solution.py:15
  98.5 5.6 %collective-permute-start.14 = (s32[20]{0:T(128)S(1)}, s32[20]{0:T(128)S(1)}, u32[]{:S(2)}, u32[]{:S(2)}) collective-permute-start(s32[20]{0:T(128)S(1)} %collective-permute-done.6), channel_id=1, source_target_pairs={{16,0},{32,16},{48,32},{64,48},{80,64},{96,80},{112,96},{128,112},... | collective-permute-start | bytes 248 | tf_op jit(solution)/shard_map/ppermute | solution.py:15
  104.8 5.7 %collective-permute-start.12 = (s32[20]{0:T(128)S(1)}, s32[20]{0:T(128)S(1)}, u32[]{:S(2)}, u32[]{:S(2)}) collective-permute-start(s32[20]{0:T(128)S(1)} %collective-permute-done.4), channel_id=1, source_target_pairs={{16,0},{32,16},{48,32},{64,48},{80,64},{96,80},{112,96},{128,112},... | collective-permute-start | bytes 248 | tf_op jit(solution)/shard_map/ppermute | solution.py:15
  111.2 5.7 %collective-permute-start.22 = (s32[20]{0:T(128)S(1)}, s32[20]{0:T(128)S(1)}, u32[]{:S(2)}, u32[]{:S(2)}) collective-permute-start(s32[20]{0:T(128)S(1)} %collective-permute-done.14), channel_id=1, source_target_pairs={{16,0},{32,16},{48,32},{64,48},{80,64},{96,80},{112,96},{128,112},... | collective-permute-start | bytes 248 | tf_op jit(solution)/shard_map/ppermute | solution.py:15
  117.6 5.7 %collective-permute-start.20 = (s32[20]{0:T(128)S(1)}, s32[20]{0:T(128)S(1)}, u32[]{:S(2)}, u32[]{:S(2)}) collective-permute-start(s32[20]{0:T(128)S(1)} %collective-permute-done.12), channel_id=1, source_target_pairs={{16,0},{32,16},{48,32},{64,48},{80,64},{96,80},{112,96},{128,112},... | collective-permute-start | bytes 248 | tf_op jit(solution)/shard_map/ppermute | solution.py:15
  123.3 1.9 collective-permute-start.11
  127.2 1.9 collective-permute-start.10
  129.2 35.3 %collective-permute-done.8 = s32[80]{0:T(128)S(1)} collective-permute-done((s32[80]{0:T(128)S(1)}, s32[80]{0:T(128)S(1)}, u32[]{:S(2)}, u32[]{:S(2)}) %collective-permute-start.8) | collective-permute-done | bytes 352 | tf_op jit(solution)/shard_map/ppermute | solution.py:15
  168.4 1.9 collective-permute-start.15
  170.4 2.6 %collective-permute-done.16 = s32[80]{0:T(128)S(1)} collective-permute-done((s32[80]{0:T(128)S(1)}, s32[80]{0:T(128)S(1)}, u32[]{:S(2)}, u32[]{:S(2)}) %collective-permute-start.16) | collective-permute-done | bytes 352 | tf_op jit(solution)/shard_map/ppermute | solution.py:15
  173.0 1.9 collective-permute-done.18
  175.0 8.3 %collective-permute-done.15 = bf16[20,128,128]{2,1,0:T(8,128)(2,1)} collective-permute-done((bf16[20,128,128]{2,1,0:T(8,128)(2,1)S(1)}, bf16[20,128,128]{2,1,0:T(8,128)(2,1)}, u32[]{:S(2)}, u32[]{:S(2)}) %collective-permute-start.15) | collective-permute-done | bytes 655392 | tf_op jit(solution)/shard_map/ppermute | solution.py:15
  183.3 2.2 collective-permute-start.23
  186.2 2.3 copy.16
  191.9 1.9 collective-permute-start.19
  196.8 2.4 %copy.24 = bf16[16,128,2,128]{1,0,3,2:T(8,128)(2,1)} copy(bf16[16,128,2,128]{3,0,1,2:T(8,128)(2,1)S(1)} %fusion.19) | data formatting | bytes 2097152 | tf_op jit(solution)/shard_map/convert_element_type | solution.py:43
  199.2 4.3 %convolution_convert_fusion.2 = bf16[8,16,128,128]{3,1,2,0:T(8,128)(2,1)S(1)} fusion(f32[80,16]{0,1:T(8,128)S(1)} %fusion.74, f32[80,8]{0,1:T(8,128)S(1)} %fusion.81, bf16[10,8,128,128]{3,2,1,0:T(8,128)(2,1)} %bitcast.124), kind=kOutput, calls=%fused_computation.14 | convolution fusion | flops 337661952 | bytes 6823424 | tf_op jit(solution)/shard_map/dot_general | solution.py:37
  207.0 4.2 %convolution_convert_fusion.1 = bf16[8,16,128,128]{3,1,2,0:T(8,128)(2,1)S(1)} fusion(f32[80,16]{0,1:T(8,128)S(1)} %fusion.76, f32[80,8]{0,1:T(8,128)S(1)} %fusion.82, bf16[10,8,128,128]{3,2,1,0:T(8,128)(2,1)} %bitcast.142), kind=kOutput, calls=%fused_computation.13 | convolution fusion | flops 337661952 | bytes 6823424 | tf_op jit(solution)/shard_map/dot_general | solution.py:37
  212.5 22.6 %collective-permute-done.19 = bf16[80,128,128]{2,1,0:T(8,128)(2,1)} collective-permute-done((bf16[80,128,128]{2,1,0:T(8,128)(2,1)}, bf16[80,128,128]{2,1,0:T(8,128)(2,1)}, u32[]{:S(2)}, u32[]{:S(2)}) %collective-permute-start.19) | collective-permute-done | bytes 2621472 | tf_op jit(solution)/shard_map/ppermute | solution.py:15
  235.1 4.3 %convolution_convert_fusion = bf16[8,16,128,128]{3,1,2,0:T(8,128)(2,1)S(1)} fusion(f32[80,16]{0,1:T(8,128)S(1)} %fusion.78, f32[80,8]{0,1:T(8,128)S(1)} %fusion.83, bf16[10,8,128,128]{3,2,1,0:T(8,128)(2,1)} %bitcast.160), kind=kOutput, calls=%fused_computation.12 | convolution fusion | flops 337661952 | bytes 6823424 | tf_op jit(solution)/shard_map/dot_general | solution.py:37
  239.4 2.1 fusion.29
  (74 shorter events, 36.2 us)
Async XLA Ops:
  0.0 98.5 %collective-permute-start.4 = (s32[20]{0:T(128)}, s32[20]{0:T(128)S(1)}, u32[]{:S(2)}, u32[]{:S(2)}) collective-permute-start(s32[20]{0:T(128)} %bitcast.292), channel_id=1, source_target_pairs={{16,0},{32,16},{48,32},{64,48},{80,64},{96,80},{112,96},{128,112},... | collective-permute-start | bytes 248 | tf_op jit(solution)/shard_map/ppermute | solution.py:15
  12.0 23.9 %collective-permute-start.5 = (s32[]{:T(128)}, s32[]{:T(128)}, u32[]{:S(2)}, u32[]{:S(2)}) collective-permute-start(s32[]{:T(128)} %bitcast.12), channel_id=1, source_target_pairs={{16,0},{32,16},{48,32},{64,48},{80,64},{96,80},{112,96},{128,112},... | collective-permute-start | bytes 20 | tf_op jit(solution)/shard_map/ppermute | solution.py:15
  14.7 81.8 %collective-permute-start.6 = (s32[20]{0:T(128)}, s32[20]{0:T(128)S(1)}, u32[]{:S(2)}, u32[]{:S(2)}) collective-permute-start(s32[20]{0:T(128)} %bitcast.298), channel_id=1, source_target_pairs={{16,0},{32,16},{48,32},{64,48},{80,64},{96,80},{112,96},{128,112},... | collective-permute-start | bytes 248 | tf_op jit(solution)/shard_map/ppermute | solution.py:15
  17.3 151.1 %collective-permute-start.7 = (bf16[20,128,128]{2,1,0:T(8,128)(2,1)}, bf16[20,128,128]{2,1,0:T(8,128)(2,1)S(1)}, u32[]{:S(2)}, u32[]{:S(2)}) collective-permute-start(bf16[20,128,128]{2,1,0:T(8,128)(2,1)} %bitcast.290), channel_id=1, source_target_pairs={{16,0},{32,16},{48,32},{64,48},{80,64},{96,80},{112,96},{128,112},... | collective-permute-start | bytes 1966088 | tf_op jit(solution)/shard_map/ppermute | solution.py:15
  20.0 103.3 %collective-permute-start.3 = (bf16[80,128,128]{2,1,0:T(8,128)(2,1)}, bf16[80,128,128]{2,1,0:T(8,128)(2,1)}, u32[]{:S(2)}, u32[]{:S(2)}) collective-permute-start(bf16[80,128,128]{2,1,0:T(8,128)(2,1)} %bitcast.284), channel_id=1, source_target_pairs={{1,0},{2,1},{3,2},{4,3},{5,4},{6,5},{7,6},{8,7},{9,8},{10,9},{11,1... | collective-permute-start | bytes 7864328 | tf_op jit(solution)/shard_map/ppermute | solution.py:15
  25.0 4.1 %copy-start.4 = (s32[1,1,80]{2,1,0:T(1,128)S(1)}, s32[1,1,80]{2,1,0:T(1,128)}, u32[]{:S(2)}) copy-start(s32[1,1,80]{2,1,0:T(1,128)} %param.10) | copy-start | bytes 964
  25.0 4.8 %copy-start.3 = (s32[1,1,80]{2,1,0:T(1,128)S(1)}, s32[1,1,80]{2,1,0:T(1,128)}, u32[]{:S(2)}) copy-start(s32[1,1,80]{2,1,0:T(1,128)} %param.9) | copy-start | bytes 964
  35.9 20.9 %collective-permute-start.1 = (s32[]{:T(128)}, s32[]{:T(128)}, u32[]{:S(2)}, u32[]{:S(2)}) collective-permute-start(s32[]{:T(128)} %bitcast.1), channel_id=1, source_target_pairs={{1,0},{2,1},{3,2},{4,3},{5,4},{6,5},{7,6},{8,7},{9,8},{10,9},{11,1... | collective-permute-start | bytes 20 | tf_op jit(solution)/shard_map/ppermute | solution.py:15
  56.9 13.5 %collective-permute-start.13 = (s32[]{:T(128)}, s32[]{:T(128)}, u32[]{:S(2)}, u32[]{:S(2)}) collective-permute-start(s32[]{:T(128)} %collective-permute-done.5), channel_id=1, source_target_pairs={{16,0},{32,16},{48,32},{64,48},{80,64},{96,80},{112,96},{128,112},... | collective-permute-start | bytes 20 | tf_op jit(solution)/shard_map/ppermute | solution.py:15
  70.3 8.8 %collective-permute-start.9 = (s32[]{:T(128)}, s32[]{:T(128)}, u32[]{:S(2)}, u32[]{:S(2)}) collective-permute-start(s32[]{:T(128)} %collective-permute-done.1), channel_id=1, source_target_pairs={{1,0},{2,1},{3,2},{4,3},{5,4},{6,5},{7,6},{8,7},{9,8},{10,9},{11,1... | collective-permute-start | bytes 20 | tf_op jit(solution)/shard_map/ppermute | solution.py:15
  79.1 6.4 %collective-permute-start.21 = (s32[]{:T(128)}, s32[]{:T(128)}, u32[]{:S(2)}, u32[]{:S(2)}) collective-permute-start(s32[]{:T(128)} %collective-permute-done.13), channel_id=1, source_target_pairs={{16,0},{32,16},{48,32},{64,48},{80,64},{96,80},{112,96},{128,112},... | collective-permute-start | bytes 20 | tf_op jit(solution)/shard_map/ppermute | solution.py:15
  85.5 8.5 %collective-permute-start.17 = (s32[]{:T(128)}, s32[]{:T(128)}, u32[]{:S(2)}, u32[]{:S(2)}) collective-permute-start(s32[]{:T(128)} %collective-permute-done.9), channel_id=1, source_target_pairs={{1,0},{2,1},{3,2},{4,3},{5,4},{6,5},{7,6},{8,7},{9,8},{10,9},{11,1... | collective-permute-start | bytes 20 | tf_op jit(solution)/shard_map/ppermute | solution.py:15
  94.0 31.3 %collective-permute-start = (s32[80]{0:T(128)S(1)}, s32[80]{0:T(128)S(1)}, u32[]{:S(2)}, u32[]{:S(2)}) collective-permute-start(s32[80]{0:T(128)S(1)} %bitcast.295), channel_id=1, source_target_pairs={{1,0},{2,1},{3,2},{4,3},{5,4},{6,5},{7,6},{8,7},{9,8},{10,9},{11,1... | collective-permute-start | bytes 968 | tf_op jit(solution)/shard_map/ppermute | solution.py:15
  96.5 30.7 %collective-permute-start.2 = (s32[80]{0:T(128)S(1)}, s32[80]{0:T(128)S(1)}, u32[]{:S(2)}, u32[]{:S(2)}) collective-permute-start(s32[80]{0:T(128)S(1)} %bitcast.297), channel_id=1, source_target_pairs={{1,0},{2,1},{3,2},{4,3},{5,4},{6,5},{7,6},{8,7},{9,8},{10,9},{11,1... | collective-permute-start | bytes 968 | tf_op jit(solution)/shard_map/ppermute | solution.py:15
  98.5 6.3 %collective-permute-start.14 = (s32[20]{0:T(128)S(1)}, s32[20]{0:T(128)S(1)}, u32[]{:S(2)}, u32[]{:S(2)}) collective-permute-start(s32[20]{0:T(128)S(1)} %collective-permute-done.6), channel_id=1, source_target_pairs={{16,0},{32,16},{48,32},{64,48},{80,64},{96,80},{112,96},{128,112},... | collective-permute-start | bytes 248 | tf_op jit(solution)/shard_map/ppermute | solution.py:15
  104.8 6.4 %collective-permute-start.12 = (s32[20]{0:T(128)S(1)}, s32[20]{0:T(128)S(1)}, u32[]{:S(2)}, u32[]{:S(2)}) collective-permute-start(s32[20]{0:T(128)S(1)} %collective-permute-done.4), channel_id=1, source_target_pairs={{16,0},{32,16},{48,32},{64,48},{80,64},{96,80},{112,96},{128,112},... | collective-permute-start | bytes 248 | tf_op jit(solution)/shard_map/ppermute | solution.py:15
  111.2 6.4 %collective-permute-start.22 = (s32[20]{0:T(128)S(1)}, s32[20]{0:T(128)S(1)}, u32[]{:S(2)}, u32[]{:S(2)}) collective-permute-start(s32[20]{0:T(128)S(1)} %collective-permute-done.14), channel_id=1, source_target_pairs={{16,0},{32,16},{48,32},{64,48},{80,64},{96,80},{112,96},{128,112},... | collective-permute-start | bytes 248 | tf_op jit(solution)/shard_map/ppermute | solution.py:15
  117.6 7.6 %collective-permute-start.20 = (s32[20]{0:T(128)S(1)}, s32[20]{0:T(128)S(1)}, u32[]{:S(2)}, u32[]{:S(2)}) collective-permute-start(s32[20]{0:T(128)S(1)} %collective-permute-done.12), channel_id=1, source_target_pairs={{16,0},{32,16},{48,32},{64,48},{80,64},{96,80},{112,96},{128,112},... | collective-permute-start | bytes 248 | tf_op jit(solution)/shard_map/ppermute | solution.py:15
  123.3 68.6 %collective-permute-start.11 = (bf16[80,128,128]{2,1,0:T(8,128)(2,1)}, bf16[80,128,128]{2,1,0:T(8,128)(2,1)}, u32[]{:S(2)}, u32[]{:S(2)}) collective-permute-start(bf16[80,128,128]{2,1,0:T(8,128)(2,1)} %collective-permute-done.3), channel_id=1, source_target_pairs={{1,0},{2,1},{3,2},{4,3},{5,4},{6,5},{7,6},{8,7},{9,8},{10,9},{11,1... | collective-permute-start | bytes 7864328 | tf_op jit(solution)/shard_map/ppermute | solution.py:15
  125.3 39.2 %collective-permute-start.8 = (s32[80]{0:T(128)S(1)}, s32[80]{0:T(128)S(1)}, u32[]{:S(2)}, u32[]{:S(2)}) collective-permute-start(s32[80]{0:T(128)S(1)} %collective-permute-done), channel_id=1, source_target_pairs={{1,0},{2,1},{3,2},{4,3},{5,4},{6,5},{7,6},{8,7},{9,8},{10,9},{11,1... | collective-permute-start | bytes 968 | tf_op jit(solution)/shard_map/ppermute | solution.py:15
  127.2 39.2 %collective-permute-start.10 = (s32[80]{0:T(128)S(1)}, s32[80]{0:T(128)S(1)}, u32[]{:S(2)}, u32[]{:S(2)}) collective-permute-start(s32[80]{0:T(128)S(1)} %collective-permute-done.2), channel_id=1, source_target_pairs={{1,0},{2,1},{3,2},{4,3},{5,4},{6,5},{7,6},{8,7},{9,8},{10,9},{11,1... | collective-permute-start | bytes 968 | tf_op jit(solution)/shard_map/ppermute | solution.py:15
  164.5 8.5 %collective-permute-start.16 = (s32[80]{0:T(128)S(1)}, s32[80]{0:T(128)S(1)}, u32[]{:S(2)}, u32[]{:S(2)}) collective-permute-start(s32[80]{0:T(128)S(1)} %collective-permute-done.8), channel_id=1, source_target_pairs={{1,0},{2,1},{3,2},{4,3},{5,4},{6,5},{7,6},{8,7},{9,8},{10,9},{11,1... | collective-permute-start | bytes 968 | tf_op jit(solution)/shard_map/ppermute | solution.py:15
  166.5 8.5 %collective-permute-start.18 = (s32[80]{0:T(128)S(1)}, s32[80]{0:T(128)S(1)}, u32[]{:S(2)}, u32[]{:S(2)}) collective-permute-start(s32[80]{0:T(128)S(1)} %collective-permute-done.10), channel_id=1, source_target_pairs={{1,0},{2,1},{3,2},{4,3},{5,4},{6,5},{7,6},{8,7},{9,8},{10,9},{11,1... | collective-permute-start | bytes 968 | tf_op jit(solution)/shard_map/ppermute | solution.py:15
  168.4 14.9 %collective-permute-start.15 = (bf16[20,128,128]{2,1,0:T(8,128)(2,1)S(1)}, bf16[20,128,128]{2,1,0:T(8,128)(2,1)}, u32[]{:S(2)}, u32[]{:S(2)}) collective-permute-start(bf16[20,128,128]{2,1,0:T(8,128)(2,1)S(1)} %collective-permute-done.7), channel_id=1, source_target_pairs={{16,0},{32,16},{48,32},{64,48},{80,64},{96,80},{112,96},{128,112},... | collective-permute-start | bytes 1966088 | tf_op jit(solution)/shard_map/ppermute | solution.py:15
  183.3 11.6 %collective-permute-start.23 = (bf16[20,128,128]{2,1,0:T(8,128)(2,1)}, bf16[20,128,128]{2,1,0:T(8,128)(2,1)}, u32[]{:S(2)}, u32[]{:S(2)}) collective-permute-start(bf16[20,128,128]{2,1,0:T(8,128)(2,1)} %collective-permute-done.15), channel_id=1, source_target_pairs={{16,0},{32,16},{48,32},{64,48},{80,64},{96,80},{112,96},{128,112},... | collective-permute-start | bytes 1966088 | tf_op jit(solution)/shard_map/ppermute | solution.py:15
  191.9 43.2 %collective-permute-start.19 = (bf16[80,128,128]{2,1,0:T(8,128)(2,1)}, bf16[80,128,128]{2,1,0:T(8,128)(2,1)}, u32[]{:S(2)}, u32[]{:S(2)}) collective-permute-start(bf16[80,128,128]{2,1,0:T(8,128)(2,1)} %collective-permute-done.11), channel_id=1, source_target_pairs={{1,0},{2,1},{3,2},{4,3},{5,4},{6,5},{7,6},{8,7},{9,8},{10,9},{11,1... | collective-permute-start | bytes 7864328 | tf_op jit(solution)/shard_map/ppermute | solution.py:15
  199.2 4.3 %copy-start.1 = (bf16[16,128,2,128]{1,0,3,2:T(8,128)(2,1)S(1)}, bf16[16,128,2,128]{1,0,3,2:T(8,128)(2,1)}, u32[]{:S(2)}) copy-start(bf16[16,128,2,128]{1,0,3,2:T(8,128)(2,1)} %copy.16) | copy-start | bytes 3145732
  203.5 2.2 copy-start
  235.1 4.3 %copy-start.2 = (bf16[16,128,2,128]{1,0,3,2:T(8,128)(2,1)S(1)}, bf16[16,128,2,128]{1,0,3,2:T(8,128)(2,1)}, u32[]{:S(2)}) copy-start(bf16[16,128,2,128]{1,0,3,2:T(8,128)(2,1)} %copy.24) | copy-start | bytes 3145732
where the time goes:
time: 243 us; the launch traced here: 242 us
  waiting for transfers between devices  105 us (43%)
  starting transfers between devices  89.7 us (37%)
  matrix products  27.6 us (11%)
  local copies, waits for them, and re-layouts  12.2 us (5%)
  other arithmetic  5.13 us (2%)
    ppermute x24, waiting for transfers between devices, passed_along(): return lax.ppermute(block, axis, route)  105 us
    ppermute x24, starting transfers between devices, passed_along(): return lax.ppermute(block, axis, route)  89.7 us
    dot_general x8, matrix products, densify(): jnp.dot(pair_hot.astype(jnp.bfloat16).T, blocks.reshape(slot_count, size...  21.7 us
    convert_element_type x4, local copies, waits for them, and re-layouts, densify(): placed.reshape(block_rows * size, block_cols * size).astype(jnp.bfloat16)  7.78 us
    dot_general x4, matrix products, panel_product(): return jnp.dot(a_dense, b_dense, preferred_element_type=jnp.float32)  5.96 us
  transfers between devices with their start and end apart: 24, of which 14 were waited for; matrix products, arithmetic and copies ran while one was open for 16% of the time, Pallas kernels for 0%

commit v1 on v0

v1 whole, which is shorter than its diff:
```python
import functools

import jax
import jax.numpy as jnp
from jax import lax
from jax.experimental import pallas as pl
from jax.experimental.pallas import tpu as pltpu
from jax.sharding import PartitionSpec as P

RB = 8
KB = 16
CB = 2
STEPS = 4
CHUNKS = 4
TILES = 4
WIDE = False

MESH = pl.DeviceIdType.MESH


def slot_codes(rows_ref, cols_ref, count_ref, block_cols):
    slots = lax.broadcasted_iota(jnp.int32, rows_ref.shape, 1)
    codes = rows_ref[...] * block_cols + cols_ref[...]
    return jnp.where(slots < count_ref[0, 0], codes, -1)


def slot_of_block(codes, blocks, empty):
    width = codes.shape[1]
    wanted = lax.broadcasted_iota(jnp.int32, (blocks, width), 0)
    slots = lax.broadcasted_iota(jnp.int32, (blocks, width), 1)
    hits = jnp.where(jnp.broadcast_to(codes, (blocks, width)) == wanted, slots, empty)
    return jnp.broadcast_to(jnp.min(hits, axis=1, keepdims=True), (blocks, 128))


def kernel(
    grid_rows,
    grid_cols,
    a_rows,
    a_cols,
    a_count,
    b_rows,
    b_cols,
    b_count,
    a_blocks,
    b_blocks,
    out_ref,
    a_held,
    a_dense,
    b_own,
    b_one,
    b_two,
    b_three,
    b_dense,
    codes,
    found_a,
    found_b,
    where_a,
    where_b,
    total,
    t_out,
    t_in,
    scale_out,
    scale_in,
    local_sem,
    b_send,
    b_recv,
    t_send,
    t_recv,
):
    pad_a, bs = a_blocks.shape[0], a_blocks.shape[1]
    pad_b = b_blocks.shape[0]
    part = pad_b // CHUNKS
    tile = RB * bs // TILES
    b_held = (b_own, b_one, b_two, b_three)
    i, k = lax.axis_index("row"), lax.axis_index("col")

    def at_col(distance):
        return (i, lax.rem(k + distance + grid_cols, grid_cols))

    onward = (lax.rem(i + grid_rows - 1, grid_rows), lax.rem(k + 1, grid_cols))
    origin = (lax.rem(i + 1, grid_rows), lax.rem(k + grid_cols - 1, grid_cols))

    a_held[pad_a] = jnp.zeros((bs, bs), jnp.bfloat16)
    for held in b_held:
        held[pad_b] = jnp.zeros((bs, bs), jnp.bfloat16)

    barrier = pltpu.get_barrier_semaphore()
    pl.semaphore_signal(barrier, inc=1, device_id=origin, device_id_type=MESH)
    for s in range(1, STEPS):
        pl.semaphore_signal(barrier, inc=1, device_id=at_col(s), device_id_type=MESH)

    b_load = pltpu.make_async_copy(b_blocks, b_own.at[pl.ds(0, pad_b)], local_sem.at[0])
    b_load.start()
    a_load = pltpu.make_async_copy(a_blocks, a_held.at[pl.ds(0, pad_a)], local_sem.at[1])
    a_load.start()

    codes[0] = jnp.full((8, 128), -1, jnp.int32)
    codes[0, 0:1, 0:pad_b] = slot_codes(b_rows, b_cols, b_count, CB)

    def code_hop(s):
        return pltpu.make_async_remote_copy(
            src_ref=codes.at[s],
            dst_ref=codes.at[s + 1],
            send_sem=b_send.at[s, CHUNKS],
            recv_sem=b_recv.at[s, CHUNKS],
            device_id=onward,
            device_id_type=MESH,
        )

    def chunk_hop(s, c):
        span = pl.ds(c * part, part)
        return pltpu.make_async_remote_copy(
            src_ref=b_blocks.at[span] if s == 0 else b_held[s].at[span],
            dst_ref=b_held[s + 1].at[span],
            send_sem=b_send.at[s, c],
            recv_sem=b_recv.at[s, c],
            device_id=onward,
            device_id_type=MESH,
        )

    def tile_home(s, t):
        span = pl.ds(pl.multiple_of(t * tile, tile), tile)
        return pltpu.make_async_remote_copy(
            src_ref=t_out.at[s - 1, span],
            dst_ref=t_in.at[s - 1, span],
            send_sem=t_send.at[s - 1, t, 0],
            recv_sem=t_recv.at[s - 1, t, 0],
            device_id=at_col(-s),
            device_id_type=MESH,
        )

    def scale_home(s, t):
        return pltpu.make_async_remote_copy(
            src_ref=scale_out.at[s - 1, t],
            dst_ref=scale_in.at[s - 1, t],
            send_sem=t_send.at[s - 1, t, 1],
            recv_sem=t_recv.at[s - 1, t, 1],
            device_id=at_col(-s),
            device_id_type=MESH,
        )

    pl.semaphore_wait(barrier, STEPS)
    code_hop(0).start()
    for c in range(CHUNKS):
        chunk_hop(0, c).start()

    found_a[...] = slot_of_block(slot_codes(a_rows, a_cols, a_count, KB), RB * KB, pad_a)
    a_table = pltpu.make_async_copy(found_a, where_a, local_sem.at[2])
    a_table.start()
    a_table.wait()
    a_load.wait()

    def place_a(p, carry):
        r, c = p // KB, p % KB
        a_dense[
            pl.ds(pl.multiple_of(r * bs, bs), bs), pl.ds(pl.multiple_of(c * bs, bs), bs)
        ] = a_held[where_a[p, 0]]
        return carry

    lax.fori_loop(0, RB * KB, place_a, 0)

    def dense_b(s):
        found_b[...] = slot_of_block(codes[s, 0:1, :], KB * CB, pad_b)
        b_table = pltpu.make_async_copy(found_b, where_b, local_sem.at[3])
        b_table.start()
        b_table.wait()

        def place_b(p, carry):
            r, c = p // CB, p % CB
            b_dense[
                pl.ds(pl.multiple_of(r * bs, bs), bs), pl.ds(pl.multiple_of(c * bs, bs), bs)
            ] = b_held[s][where_b[p, 0]]
            return carry

        lax.fori_loop(0, KB * CB, place_b, 0)

    def product(t):
        rows = pl.ds(pl.multiple_of(t * tile, tile), tile)
        return jnp.dot(a_dense[rows, :], b_dense[...], preferred_element_type=jnp.float32)

    def own_tile(t, carry):
        rows = pl.ds(pl.multiple_of(t * tile, tile), tile)
        total[rows, :] = product(t)
        return carry

    b_load.wait()
    dense_b(0)
    lax.fori_loop(0, TILES, own_tile, 0)

    def term_from(s, t):
        rows = pl.ds(pl.multiple_of(t * tile, tile), tile)
        tile_home(s, t).wait_recv()
        if WIDE:
            return t_in[s - 1, rows, :]
        scale_home(s, t).wait_recv()
        return t_in[s - 1, rows, :].astype(jnp.float32) * scale_in[s - 1, t]

    def add_tile(s, t, carry):
        rows = pl.ds(pl.multiple_of(t * tile, tile), tile)
        total[rows, :] = total[rows, :] + term_from(s, t)
        return carry

    def last_tile(t, carry):
        rows = pl.ds(pl.multiple_of(t * tile, tile), tile)
        out_ref[rows, :] = (total[rows, :] + term_from(STEPS - 1, t)).astype(jnp.bfloat16)
        return carry

    def sent_tile(s, t, carry):
        rows = pl.ds(pl.multiple_of(t * tile, tile), tile)
        term = product(t)
        if WIDE:
            t_out[s - 1, rows, :] = term
        else:
            largest = jnp.maximum(jnp.max(jnp.abs(term), axis=0, keepdims=True), 1e-30)
            scale_out[s - 1, t] = largest * (1.0 / 32767.0)
            scale_home(s, t).start()
            coded = jnp.round(term * (32767.0 / largest))
            t_out[s - 1, rows, :] = coded.astype(jnp.int32).astype(jnp.int16)
        tile_home(s, t).start()
        return carry

    for s in range(1, STEPS):
        code_hop(s - 1).wait_recv()
        if s < STEPS - 1:
            code_hop(s).start()
        for c in range(CHUNKS):
            chunk_hop(s - 1, c).wait_recv()
            if s < STEPS - 1:
                chunk_hop(s, c).start()
        dense_b(s)
        lax.fori_loop(0, TILES, functools.partial(sent_tile, s), 0)
        if s > 1:
            lax.fori_loop(0, TILES, functools.partial(add_tile, s - 1), 0)
    lax.fori_loop(0, TILES, last_tile, 0)

    for s in range(STEPS - 1):
        code_hop(s).wait_send()
        for c in range(CHUNKS):
            chunk_hop(s, c).wait_send()
        for t in range(TILES):
            tile_home(s + 1, t).wait_send()
            if not WIDE:
                scale_home(s + 1, t).wait_send()


def per_device(a_blocks, a_rows, a_cols, a_count, b_blocks, b_rows, b_cols, b_count):
    grid_rows, grid_cols = lax.axis_size("row"), lax.axis_size("col")
    pad_a, bs = a_blocks.shape[2], a_blocks.shape[3]
    pad_b = b_blocks.shape[2]
    sent = jnp.float32 if WIDE else jnp.int16
    vmem = pl.BlockSpec(memory_space=pltpu.VMEM)
    smem = pl.BlockSpec(memory_space=pltpu.SMEM)
    whole = pl.BlockSpec(memory_space=pl.ANY)
    rows, depth, columns = RB * bs, KB * bs, CB * bs
    return pl.pallas_call(
        functools.partial(kernel, grid_rows, grid_cols),
        out_shape=jax.ShapeDtypeStruct((rows, columns), jnp.bfloat16),
        in_specs=[vmem, vmem, smem, vmem, vmem, smem, whole, whole],
        out_specs=vmem,
        scratch_shapes=[
            pltpu.VMEM((pad_a + 1, bs, bs), jnp.bfloat16),
            pltpu.VMEM((rows, depth), jnp.bfloat16),
            *[pltpu.VMEM((pad_b + 1, bs, bs), jnp.bfloat16)] * STEPS,
            pltpu.VMEM((depth, columns), jnp.bfloat16),
            pltpu.VMEM((STEPS, 8, 128), jnp.int32),
            pltpu.VMEM((RB * KB, 128), jnp.int32),
            pltpu.VMEM((KB * CB, 128), jnp.int32),
            pltpu.SMEM((RB * KB, 128), jnp.int32),
            pltpu.SMEM((KB * CB, 128), jnp.int32),
            pltpu.VMEM((rows, columns), jnp.float32),
            pltpu.VMEM((STEPS - 1, rows, columns), sent),
            pltpu.VMEM((STEPS - 1, rows, columns), sent),
            pltpu.VMEM((STEPS - 1, TILES, 1, columns), jnp.float32),
            pltpu.VMEM((STEPS - 1, TILES, 1, columns), jnp.float32),
            pltpu.SemaphoreType.DMA((4,)),
            pltpu.SemaphoreType.DMA((STEPS - 1, CHUNKS + 1)),
            pltpu.SemaphoreType.DMA((STEPS - 1, CHUNKS + 1)),
            pltpu.SemaphoreType.DMA((STEPS - 1, TILES, 2)),
            pltpu.SemaphoreType.DMA((STEPS - 1, TILES, 2)),
        ],
        compiler_params=pltpu.CompilerParams(
            collective_id=0, has_side_effects=True, vmem_limit_bytes=48 * 1024 * 1024
        ),
    )(
        a_rows.reshape(1, pad_a),
        a_cols.reshape(1, pad_a),
        a_count,
        b_rows.reshape(1, pad_b),
        b_cols.reshape(1, pad_b),
        b_count,
        a_blocks.reshape(pad_a, bs, bs),
        b_blocks.reshape(pad_b, bs, bs),
    )


def solution(mesh):
    placed = (
        P("row", "col", None, None, None),
        P("row", "col", None),
        P("row", "col", None),
        P("row", "col"),
        P("row", "col", None, None, None),
        P("row", "col", None),
        P("row", "col", None),
        P("row", "col"),
    )
    return jax.shard_map(
        per_device, mesh=mesh, in_specs=placed, out_specs=P("row", "col"), check_vma=False
    )
```

time: 243 us -> 92.7 us (0.38)
  the two profiles are of different devices: /device:TPU:25 before, /device:TPU:497 now
where the time goes in v1:
time: 92.7 us; the launch traced here: 92.5 us
  Pallas kernels  84.9 us (92%)
  local copies, waits for them, and re-layouts  6.23 us (7%)
  between operations  1.32 us (1%)
    pallas_call x1, Pallas kernels, per_device(): pl.pallas_call(functools.partial(kernel, grid_rows, grid_cols), out_shape...  84.9 us
    unnamed x13, local copies, waits for them, and re-layouts  6.23 us

profile of v1, /device:TPU:497, one launch (start us, length us, event | category | flops | bytes accessed | tf_op | source)
XLA Modules:
  0.0 92.5 jit_solution(8137515323114213638)
XLA Ops:
  1.3 0.0 copy-start
  1.3 1.7 %copy-done = bf16[1,1,80,128,128]{4,3,2,1,0:T(8,128)(2,1)S(1)} copy-done((bf16[1,1,80,128,128]{4,3,2,1,0:T(8,128)(2,1)S(1)}, bf16[1,1,80,128,128]{4,3,2,1,0:T(8,128)(2,1)}, u32[]{:S(2)}) %copy-start) | copy-done | bytes 2621464
  3.0 0.0 copy-start.1
  3.0 1.1 %copy-done.1 = bf16[1,1,20,128,128]{4,3,2,1,0:T(8,128)(2,1)S(1)} copy-done((bf16[1,1,20,128,128]{4,3,2,1,0:T(8,128)(2,1)S(1)}, bf16[1,1,20,128,128]{4,3,2,1,0:T(8,128)(2,1)}, u32[]{:S(2)}) %copy-start.1) | copy-done | bytes 655384
  4.1 0.0 copy-start.2
  4.1 0.7 copy-done.2
  4.8 0.0 copy-start.3
  4.8 0.7 copy-done.3
  5.4 0.0 copy-start.4
  5.4 0.7 copy-done.4
  6.1 0.0 copy-start.5
  6.1 0.7 copy-done.5
  6.7 84.9 %shard_map.82 = bf16[1024,256]{1,0:T(8,128)(2,1)S(1)} custom-call(s32[1,80]{1,0:T(1,128)S(1)} %bitcast.8, s32[1,80]{1,0:T(1,128)S(1)} %bitcast.9, s32[1,1]{1,0:T(1,128)S(6)} %copy.10.a_count, s32[1,20]{1,0:T(1,128)S(1)} %bitcast.10, s32[1,20]{1,0:T(1,128)S(1)} %bitcast.11, s32[1,1]{1,0:T(1,128)S(6)} %copy.11.b_count, bf16[80,128,128]{2,1,0:T(8,128)(2,1)S(1)} %bitcast.6, ...), custom_call_target="tpu_custom_call" | custom-call | tf_op jit(solution)/shard_map/pallas_call | solution.py:255
  91.7 0.8 copy.12
Async XLA Ops:
  1.3 1.7 %copy-start = (bf16[1,1,80,128,128]{4,3,2,1,0:T(8,128)(2,1)S(1)}, bf16[1,1,80,128,128]{4,3,2,1,0:T(8,128)(2,1)}, u32[]{:S(2)}) copy-start(bf16[1,1,80,128,128]{4,3,2,1,0:T(8,128)(2,1)} %param.8) | copy-start | bytes 7864324
  3.0 1.1 %copy-start.1 = (bf16[1,1,20,128,128]{4,3,2,1,0:T(8,128)(2,1)S(1)}, bf16[1,1,20,128,128]{4,3,2,1,0:T(8,128)(2,1)}, u32[]{:S(2)}) copy-start(bf16[1,1,20,128,128]{4,3,2,1,0:T(8,128)(2,1)} %param.12) | copy-start | bytes 1966084
  4.1 0.7 copy-start.2
  4.8 0.7 copy-start.3
  5.4 0.7 copy-start.4
  6.1 0.7 copy-start.5

commit v2 on v1

v2 whole, which is shorter than its diff:
```python
import functools

import jax
import jax.numpy as jnp
from jax import lax
from jax.experimental import pallas as pl
from jax.experimental.pallas import tpu as pltpu
from jax.sharding import PartitionSpec as P

RB = 8
KB = 16
CB = 2
STEPS = 4
HALVES = 2
TILES = 2

MESH = pl.DeviceIdType.MESH


def slot_codes(rows_ref, cols_ref, count_ref, block_cols):
    slots = lax.broadcasted_iota(jnp.int32, rows_ref.shape, 1)
    codes = rows_ref[...] * block_cols + cols_ref[...]
    return jnp.where(slots < count_ref[0, 0], codes, -1)


def slot_of_block(codes, blocks, empty):
    width = codes.shape[1]
    wanted = lax.broadcasted_iota(jnp.int32, (blocks, width), 0)
    slots = lax.broadcasted_iota(jnp.int32, (blocks, width), 1)
    hits = jnp.where(jnp.broadcast_to(codes, (blocks, width)) == wanted, slots, empty)
    return jnp.broadcast_to(jnp.min(hits, axis=1, keepdims=True), (blocks, 128))


def kernel(
    grid_rows,
    grid_cols,
    a_rows_hbm,
    a_cols_hbm,
    a_count,
    b_rows_hbm,
    b_cols_hbm,
    b_count,
    a_blocks,
    b_blocks,
    out_ref,
    a_rows,
    a_cols,
    b_rows,
    b_cols,
    a_held,
    a_dense,
    b_raw,
    own_0,
    own_1,
    one_0,
    one_1,
    two_0,
    two_1,
    three_0,
    three_1,
    b_dense,
    codes,
    found_a,
    found_b,
    where_a,
    where_b,
    total,
    t_out,
    t_in,
    scale_out,
    scale_in,
    passed,
    local_sem,
    table_sem,
    b_send,
    b_recv,
    pass_send,
    pass_recv,
    t_send,
    t_recv,
):
    pad_a, bs = a_blocks.shape[0], a_blocks.shape[1]
    pad_b = b_blocks.shape[0]
    strip = bs // HALVES
    tile = RB * bs // TILES
    b_held = ((own_0, own_1), (one_0, one_1), (two_0, two_1), (three_0, three_1))
    i, k = lax.axis_index("row"), lax.axis_index("col")

    def at_col(distance):
        return (i, lax.rem(k + distance + grid_cols, grid_cols))

    onward = (lax.rem(i + grid_rows - 1, grid_rows), lax.rem(k + 1, grid_cols))
    origin = (lax.rem(i + 1, grid_rows), lax.rem(k + grid_cols - 1, grid_cols))

    run = grid_rows // 2
    at_first, at_last = lax.rem(i, run) == 0, lax.rem(i, run) == run - 1
    beside = (lax.rem(i + run, grid_rows), k)
    past_beside = (lax.rem(i + run + grid_rows - 1, grid_rows), lax.rem(k + 1, grid_cols))
    passes_here = (lax.rem(i + 1 + run, grid_rows), lax.rem(k + grid_cols - 1, grid_cols))

    nothing = jnp.zeros((strip, bs), jnp.bfloat16)
    for held in b_held:
        for h in range(HALVES):
            held[h][pad_b] = nothing
    a_held[pad_a] = jnp.zeros((bs, bs), jnp.bfloat16)

    barrier = pltpu.get_barrier_semaphore()
    pl.semaphore_signal(barrier, inc=1, device_id=origin, device_id_type=MESH)
    for s in range(1, STEPS):
        pl.semaphore_signal(barrier, inc=1, device_id=at_col(s), device_id_type=MESH)

    @pl.when(at_last)
    def _():
        pl.semaphore_signal(barrier, inc=1, device_id=passes_here, device_id_type=MESH)

    @pl.when(at_first)
    def _():
        pl.semaphore_signal(barrier, inc=1, device_id=beside, device_id_type=MESH)

    loads = [
        pltpu.make_async_copy(source, target, local_sem.at[n])
        for n, (source, target) in enumerate(
            (
                (b_blocks, b_raw),
                (b_rows_hbm, b_rows),
                (b_cols_hbm, b_cols),
                (a_rows_hbm, a_rows),
                (a_cols_hbm, a_cols),
                (a_blocks, a_held.at[pl.ds(0, pad_a)]),
            )
        )
    ]
    for load in loads:
        load.start()

    def code_hop(s):
        return pltpu.make_async_remote_copy(
            src_ref=codes.at[s],
            dst_ref=codes.at[s + 1],
            send_sem=b_send.at[s, HALVES],
            recv_sem=b_recv.at[s, HALVES],
            device_id=onward,
            device_id_type=MESH,
        )

    def half_hop(s, h):
        return pltpu.make_async_remote_copy(
            src_ref=b_held[s][h].at[pl.ds(0, pad_b)],
            dst_ref=b_held[s + 1][h].at[pl.ds(0, pad_b)],
            send_sem=b_send.at[s, h],
            recv_sem=b_recv.at[s, h],
            device_id=onward,
            device_id_type=MESH,
        )

    def hop_beside(s):
        return pltpu.make_async_remote_copy(
            src_ref=b_held[s][HALVES - 1].at[pl.ds(0, pad_b)],
            dst_ref=passed.at[s],
            send_sem=b_send.at[s, HALVES - 1],
            recv_sem=pass_recv.at[s],
            device_id=beside,
            device_id_type=MESH,
        )

    def pass_on(s):
        return pltpu.make_async_remote_copy(
            src_ref=passed.at[s],
            dst_ref=b_held[s + 1][HALVES - 1].at[pl.ds(0, pad_b)],
            send_sem=pass_send.at[s],
            recv_sem=b_recv.at[s, HALVES - 1],
            device_id=past_beside,
            device_id_type=MESH,
        )

    def start_half(s, h):
        if h < HALVES - 1:
            half_hop(s, h).start()
            return

        @pl.when(at_first)
        def _():
            hop_beside(s).start()

        @pl.when(jnp.logical_not(at_first))
        def _():
            half_hop(s, h).start()

    def start_pass(s):
        @pl.when(at_first)
        def _():
            hop_beside(s).wait_recv()
            pass_on(s).start()

    def tile_rows(t):
        return pl.ds(pl.multiple_of(t * tile, tile), tile)

    def tile_home(s, h, t):
        return pltpu.make_async_remote_copy(
            src_ref=t_out.at[s - 1, h, tile_rows(t)],
            dst_ref=t_in.at[s - 1, h, tile_rows(t)],
            send_sem=t_send.at[s - 1, h, t, 0],
            recv_sem=t_recv.at[s - 1, h, t, 0],
            device_id=at_col(-s),
            device_id_type=MESH,
        )

    def scale_home(s, h, t):
        return pltpu.make_async_remote_copy(
            src_ref=scale_out.at[s - 1, h, t],
            dst_ref=scale_in.at[s - 1, h, t],
            send_sem=t_send.at[s - 1, h, t, 1],
            recv_sem=t_recv.at[s - 1, h, t, 1],
            device_id=at_col(-s),
            device_id_type=MESH,
        )

    loads[0].wait()

    def turn(p, carry):
        turned = b_raw[p].T
        for h in range(HALVES):
            b_held[0][h][p] = turned[h * strip : (h + 1) * strip, :]
        return carry

    lax.fori_loop(0, pad_b, turn, 0, unroll=True)
    loads[1].wait()
    loads[2].wait()
    codes[0] = jnp.full((8, 128), -1, jnp.int32)
    codes[0, 0:1, 0:pad_b] = slot_codes(b_rows, b_cols, b_count, CB)

    pl.semaphore_wait(barrier, jnp.where(at_first, STEPS + 2, STEPS))
    code_hop(0).start()
    for h in range(HALVES):
        start_half(0, h)

    loads[3].wait()
    loads[4].wait()
    found_a[...] = slot_of_block(slot_codes(a_rows, a_cols, a_count, KB), RB * KB, pad_a)
    a_table = pltpu.make_async_copy(found_a, where_a, table_sem.at[STEPS])
    a_table.start()

    def b_table(s):
        return pltpu.make_async_copy(found_b.at[s], where_b.at[s], table_sem.at[s])

    def find_b(s):
        found_b[s] = slot_of_block(codes[s, 0:1, :], KB * CB, pad_b)
        b_table(s).start()

    find_b(0)
    a_table.wait()
    loads[5].wait()

    def place_a(p, carry):
        r, c = p // KB, p % KB
        a_dense[
            pl.ds(pl.multiple_of(r * bs, bs), bs), pl.ds(pl.multiple_of(c * bs, bs), bs)
        ] = a_held[where_a[p, 0]]
        return carry

    lax.fori_loop(0, RB * KB, place_a, 0, unroll=8)

    def place_b(s, h):
        def place(r, carry):
            for c in range(CB):
                b_dense[
                    h, c * strip : (c + 1) * strip, pl.ds(pl.multiple_of(r * bs, bs), bs)
                ] = b_held[s][h][where_b[s, r * CB + c, 0]]
            return carry

        lax.fori_loop(0, KB, place, 0, unroll=4)

    def product(h, t):
        return lax.dot_general(
            a_dense[tile_rows(t), :],
            b_dense[h],
            (((1,), (1,)), ((), ())),
            preferred_element_type=jnp.float32,
        )

    def own_tile(h, t, carry):
        total[h, tile_rows(t), :] = product(h, t)
        return carry

    def sent_tile(s, h, t, carry):
        term = product(h, t)
        largest = jnp.maximum(jnp.max(jnp.abs(term), axis=0, keepdims=True), 1e-30)
        scale_out[s - 1, h, t] = largest * (1.0 / 32767.0)
        scale_home(s, h, t).start()
        coded = jnp.round(term * (32767.0 / largest))
        t_out[s - 1, h, tile_rows(t), :] = coded.astype(jnp.int32).astype(jnp.int16)
        tile_home(s, h, t).start()
        return carry

    def term_from(s, h, t):
        scale_home(s, h, t).wait_recv()
        tile_home(s, h, t).wait_recv()
        return t_in[s - 1, h, tile_rows(t), :].astype(jnp.float32) * scale_in[s - 1, h, t]

    def add_tile(s, h, t, carry):
        total[h, tile_rows(t), :] = total[h, tile_rows(t), :] + term_from(s, h, t)
        return carry

    b_table(0).wait()
    for h in range(HALVES):
        place_b(0, h)
        lax.fori_loop(0, TILES, functools.partial(own_tile, h), 0)

    for s in range(1, STEPS):
        start_pass(s - 1)
        code_hop(s - 1).wait_recv()
        if s < STEPS - 1:
            code_hop(s).start()
        find_b(s)
        b_table(s).wait()
        for h in range(HALVES):
            half_hop(s - 1, h).wait_recv()
            if s < STEPS - 1:
                start_half(s, h)
            place_b(s, h)
            lax.fori_loop(0, TILES, functools.partial(sent_tile, s, h), 0)

    for s in range(1, STEPS):
        for h in range(HALVES):
            lax.fori_loop(0, TILES, functools.partial(add_tile, s, h), 0)

    def finish(t, carry):
        for c in range(CB):
            strips = [total[h, tile_rows(t), c * strip : (c + 1) * strip] for h in range(HALVES)]
            out_ref[tile_rows(t), c * bs : (c + 1) * bs] = jnp.concatenate(strips, axis=1).astype(jnp.bfloat16)
        return carry

    lax.fori_loop(0, TILES, finish, 0)

    @pl.when(at_first)
    def _():
        for s in range(STEPS - 1):
            pass_on(s).wait_send()

    for s in range(STEPS - 1):
        code_hop(s).wait_send()
        for h in range(HALVES):
            half_hop(s, h).wait_send()
            for t in range(TILES):
                tile_home(s + 1, h, t).wait_send()
                scale_home(s + 1, h, t).wait_send()


def per_device(a_blocks, a_rows, a_cols, a_count, b_blocks, b_rows, b_cols, b_count):
    grid_rows, grid_cols = lax.axis_size("row"), lax.axis_size("col")
    pad_a, bs = a_blocks.shape[2], a_blocks.shape[3]
    pad_b = b_blocks.shape[2]
    vmem = pl.BlockSpec(memory_space=pltpu.VMEM)
    smem = pl.BlockSpec(memory_space=pltpu.SMEM)
    whole = pl.BlockSpec(memory_space=pltpu.HBM)
    rows, depth, columns = RB * bs, KB * bs, CB * bs
    strip, wide = bs // HALVES, columns // HALVES
    return pl.pallas_call(
        functools.partial(kernel, grid_rows, grid_cols),
        out_shape=jax.ShapeDtypeStruct((rows, columns), jnp.bfloat16),
        in_specs=[whole, whole, smem, whole, whole, smem, whole, whole],
        out_specs=vmem,
        scratch_shapes=[
            pltpu.VMEM((1, pad_a), jnp.int32),
            pltpu.VMEM((1, pad_a), jnp.int32),
            pltpu.VMEM((1, pad_b), jnp.int32),
            pltpu.VMEM((1, pad_b), jnp.int32),
            pltpu.VMEM((pad_a + 1, bs, bs), jnp.bfloat16),
            pltpu.VMEM((rows, depth), jnp.bfloat16),
            pltpu.VMEM((pad_b, bs, bs), jnp.bfloat16),
            *[pltpu.VMEM((pad_b + 1, strip, bs), jnp.bfloat16)] * (STEPS * HALVES),
            pltpu.VMEM((HALVES, wide, depth), jnp.bfloat16),
            pltpu.VMEM((STEPS, 8, 128), jnp.int32),
            pltpu.VMEM((RB * KB, 128), jnp.int32),
            pltpu.VMEM((STEPS, KB * CB, 128), jnp.int32),
            pltpu.SMEM((RB * KB, 128), jnp.int32),
            pltpu.SMEM((STEPS, KB * CB, 128), jnp.int32),
            pltpu.VMEM((HALVES, rows, wide), jnp.float32),
            pltpu.VMEM((STEPS - 1, HALVES, rows, wide), jnp.int16),
            pltpu.VMEM((STEPS - 1, HALVES, rows, wide), jnp.int16),
            pltpu.VMEM((STEPS - 1, HALVES, TILES, 1, wide), jnp.float32),
            pltpu.VMEM((STEPS - 1, HALVES, TILES, 1, wide), jnp.float32),
            pltpu.VMEM((STEPS - 1, pad_b, strip, bs), jnp.bfloat16),
            pltpu.SemaphoreType.DMA((6,)),
            pltpu.SemaphoreType.DMA((STEPS + 1,)),
            pltpu.SemaphoreType.DMA((STEPS - 1, HALVES + 1)),
            pltpu.SemaphoreType.DMA((STEPS - 1, HALVES + 1)),
            pltpu.SemaphoreType.DMA((STEPS - 1,)),
            pltpu.SemaphoreType.DMA((STEPS - 1,)),
            pltpu.SemaphoreType.DMA((STEPS - 1, HALVES, TILES, 2)),
            pltpu.SemaphoreType.DMA((STEPS - 1, HALVES, TILES, 2)),
        ],
        compiler_params=pltpu.CompilerParams(
            collective_id=0, has_side_effects=True, vmem_limit_bytes=60 * 1024 * 1024
        ),
    )(
        a_rows.reshape(1, pad_a),
        a_cols.reshape(1, pad_a),
        a_count,
        b_rows.reshape(1, pad_b),
        b_cols.reshape(1, pad_b),
        b_count,
        a_blocks.reshape(pad_a, bs, bs),
        b_blocks.reshape(pad_b, bs, bs),
    )


def solution(mesh):
    placed = (
        P("row", "col", None, None, None),
        P("row", "col", None),
        P("row", "col", None),
        P("row", "col"),
        P("row", "col", None, None, None),
        P("row", "col", None),
        P("row", "col", None),
        P("row", "col"),
    )
    return jax.shard_map(
        per_device, mesh=mesh, in_specs=placed, out_specs=P("row", "col"), check_vma=False
    )
```

time: 92.7 us -> 78 us (0.84)
  the two profiles are of different devices: /device:TPU:497 before, /device:TPU:9 now
where the time goes in v2:
time: 78 us; the launch traced here: 77.9 us
  Pallas kernels  74.7 us (96%)
  local copies, waits for them, and re-layouts  1.87 us (2%)
  between operations  1.3 us (2%)
    pallas_call x1, Pallas kernels, per_device(): pl.pallas_call(functools.partial(kernel, grid_rows, grid_cols), out_shape...  74.7 us
    unnamed x1, local copies, waits for them, and re-layouts  1.87 us

profile of v2, /device:TPU:9, one launch (start us, length us, event | category | flops | bytes accessed | tf_op | source)
XLA Modules:
  0.0 77.9 jit_solution(12458576736949684670)
XLA Ops:
  1.3 74.7 %shard_map.82 = bf16[1024,256]{1,0:T(8,128)(2,1)} custom-call(s32[1,80]{1,0:T(1,128)} %bitcast.8, s32[1,80]{1,0:T(1,128)} %bitcast.9, s32[1,1]{1,0:T(1,128)S(6)} %copy.10.a_count, s32[1,20]{1,0:T(1,128)} %bitcast.10, s32[1,20]{1,0:T(1,128)} %bitcast.11, s32[1,1]{1,0:T(1,128)S(6)} %copy.11.b_count, bf16[80,128,128]{2,1,0:T(8,128)(2,1)} %bitcast.6, ...), custom_call_target="tpu_custom_call" | custom-call | tf_op jit(solution)/shard_map/pallas_call | solution.py:358
  76.0 1.9 %copy.12 = bf16[1024,256]{1,0:T(8,128)(2,1)} copy(bf16[1024,256]{1,0:T(8,128)(2,1)} %shard_map.82) | data formatting | bytes 1048576

commit v3 on v2

--- a/solution.py
+++ b/solution.py
@@ -76,6 +76,10 @@
     b_recv,
     pass_send,
     pass_recv,
+    term_held,
+    term_scale,
+    term_send,
+    term_recv,
     t_send,
     t_recv,
 ):
@@ -92,11 +96,15 @@
     onward = (lax.rem(i + grid_rows - 1, grid_rows), lax.rem(k + 1, grid_cols))
     origin = (lax.rem(i + 1, grid_rows), lax.rem(k + grid_cols - 1, grid_cols))
 
-    run = grid_rows // 2
-    at_first, at_last = lax.rem(i, run) == 0, lax.rem(i, run) == run - 1
+    run, lane = grid_rows // 2, grid_cols // 2
+
+    def passing(row, col):
+        return jnp.logical_and(lax.rem(row, run) == 0, lax.rem(col, lane) < lane - 2)
+
     beside = (lax.rem(i + run, grid_rows), k)
     past_beside = (lax.rem(i + run + grid_rows - 1, grid_rows), lax.rem(k + 1, grid_cols))
     passes_here = (lax.rem(i + 1 + run, grid_rows), lax.rem(k + grid_cols - 1, grid_cols))
+    at_first, at_last = passing(i, k), passing(*passes_here)
 
     nothing = jnp.zeros((strip, bs), jnp.bfloat16)
     for held in b_held:
@@ -106,8 +114,13 @@
 
     barrier = pltpu.get_barrier_semaphore()
     pl.semaphore_signal(barrier, inc=1, device_id=origin, device_id_type=MESH)
-    for s in range(1, STEPS):
-        pl.semaphore_signal(barrier, inc=1, device_id=at_col(s), device_id_type=MESH)
+    first_y, last_y = lax.rem(k, lane) < 2, lax.rem(k, lane) >= lane - 2
+    for distance in (1, jnp.where(last_y, lane, 2), 3):
+        pl.semaphore_signal(barrier, inc=1, device_id=at_col(distance), device_id_type=MESH)
+
+    @pl.when(last_y)
+    def _():
+        pl.semaphore_signal(barrier, inc=1, device_id=at_col(2 + lane), device_id_type=MESH)
 
     @pl.when(at_last)
     def _():
@@ -155,9 +168,9 @@
 
     def hop_beside(s):
         return pltpu.make_async_remote_copy(
-            src_ref=b_held[s][HALVES - 1].at[pl.ds(0, pad_b)],
+            src_ref=b_held[s][0].at[pl.ds(0, pad_b)],
             dst_ref=passed.at[s],
-            send_sem=b_send.at[s, HALVES - 1],
+            send_sem=b_send.at[s, 0],
             recv_sem=pass_recv.at[s],
             device_id=beside,
             device_id_type=MESH,
@@ -166,15 +179,15 @@
     def pass_on(s):
         return pltpu.make_async_remote_copy(
             src_ref=passed.at[s],
-            dst_ref=b_held[s + 1][HALVES - 1].at[pl.ds(0, pad_b)],
+            dst_ref=b_held[s + 1][0].at[pl.ds(0, pad_b)],
             send_sem=pass_send.at[s],
-            recv_sem=b_recv.at[s, HALVES - 1],
+            recv_sem=b_recv.at[s, 0],
             device_id=past_beside,
             device_id_type=MESH,
         )
 
     def start_half(s, h):
-        if h < HALVES - 1:
+        if h > 0:
             half_hop(s, h).start()
             return
 
@@ -215,6 +228,71 @@
             device_id_type=MESH,
         )
 
+    def beside_home(h, t):
+        return (
+            pltpu.make_async_remote_copy(
+                src_ref=t_out.at[1, h, tile_rows(t)],
+                dst_ref=term_held.at[h, tile_rows(t)],
+                send_sem=t_send.at[1, h, t, 0],
+                recv_sem=term_recv.at[h, t, 0],
+                device_id=at_col(lane - 2),
+                device_id_type=MESH,
+            ),
+            pltpu.make_async_remote_copy(
+                src_ref=scale_out.at[1, h, t],
+                dst_ref=term_scale.at[h, t],
+                send_sem=t_send.at[1, h, t, 1],
+                recv_sem=term_recv.at[h, t, 1],
+                device_id=at_col(lane - 2),
+                device_id_type=MESH,
+            ),
+        )
+
+    def passed_home(h, t):
+        return (
+            pltpu.make_async_remote_copy(
+                src_ref=term_held.at[h, tile_rows(t)],
+                dst_ref=t_in.at[1, h, tile_rows(t)],
+                send_sem=term_send.at[h, t, 0],
+                recv_sem=t_recv.at[1, h, t, 0],
+                device_id=at_col(lane),
+                device_id_type=MESH,
+            ),
+            pltpu.make_async_remote_copy(
+                src_ref=term_scale.at[h, t],
+                dst_ref=scale_in.at[1, h, t],
+                send_sem=term_send.at[h, t, 1],
+                recv_sem=t_recv.at[1, h, t, 1],
+                device_id=at_col(lane),
+                device_id_type=MESH,
+            ),
+        )
+
+    def start_home(s, h, t):
+        def straight():
+            scale_home(s, h, t).start()
+            tile_home(s, h, t).start()
+
+        if s != 2:
+            straight()
+            return
+
+        @pl.when(first_y)
+        def _():
+            for copy in beside_home(h, t):
+                copy.start()
+
+        pl.when(jnp.logical_not(first_y))(straight)
+
+    def pass_home(h):
+        @pl.when(last_y)
+        def _():
+            for t in range(TILES):
+                for copy in beside_home(h, t):
+                    copy.wait_recv()
+                for copy in passed_home(h, t):
+                    copy.start()
+
     loads[0].wait()
 
     def turn(p, carry):
@@ -229,7 +307,7 @@
     codes[0] = jnp.full((8, 128), -1, jnp.int32)
     codes[0, 0:1, 0:pad_b] = slot_codes(b_rows, b_cols, b_count, CB)
 
-    pl.semaphore_wait(barrier, jnp.where(at_first, STEPS + 2, STEPS))
+    pl.semaphore_wait(barrier, STEPS + jnp.where(at_first, 2, 0) + jnp.where(last_y, 1, 0))
     code_hop(0).start()
     for h in range(HALVES):
         start_half(0, h)
@@ -286,10 +364,9 @@
         term = product(h, t)
         largest = jnp.maximum(jnp.max(jnp.abs(term), axis=0, keepdims=True), 1e-30)
         scale_out[s - 1, h, t] = largest * (1.0 / 32767.0)
-        scale_home(s, h, t).start()
         coded = jnp.round(term * (32767.0 / largest))
         t_out[s - 1, h, tile_rows(t), :] = coded.astype(jnp.int32).astype(jnp.int16)
-        tile_home(s, h, t).start()
+        start_home(s, h, t)
         return carry
 
     def term_from(s, h, t):
@@ -306,8 +383,8 @@
         place_b(0, h)
         lax.fori_loop(0, TILES, functools.partial(own_tile, h), 0)
 
+    start_pass(0)
     for s in range(1, STEPS):
-        start_pass(s - 1)
         code_hop(s - 1).wait_recv()
         if s < STEPS - 1:
             code_hop(s).start()
@@ -319,6 +396,10 @@
                 start_half(s, h)
             place_b(s, h)
             lax.fori_loop(0, TILES, functools.partial(sent_tile, s, h), 0)
+            if s < STEPS - 1 and h == 0:
+                start_pass(s)
+            if s == STEPS - 1:
+                pass_home(h)
 
     for s in range(1, STEPS):
         for h in range(HALVES):
@@ -336,6 +417,13 @@
     def _():
         for s in range(STEPS - 1):
             pass_on(s).wait_send()
+
+    @pl.when(last_y)
+    def _():
+        for h in range(HALVES):
+            for t in range(TILES):
+                for copy in passed_home(h, t):
+                    copy.wait_send()
 
     for s in range(STEPS - 1):
         code_hop(s).wait_send()
@@ -387,6 +475,10 @@
             pltpu.SemaphoreType.DMA((STEPS - 1, HALVES + 1)),
             pltpu.SemaphoreType.DMA((STEPS - 1,)),
             pltpu.SemaphoreType.DMA((STEPS - 1,)),
+            pltpu.VMEM((HALVES, rows, wide), jnp.int16),
+            pltpu.VMEM((HALVES, TILES, 1, wide), jnp.float32),
+            pltpu.SemaphoreType.DMA((HALVES, TILES, 2)),
+            pltpu.SemaphoreType.DMA((HALVES, TILES, 2)),
             pltpu.SemaphoreType.DMA((STEPS - 1, HALVES, TILES, 2)),
             pltpu.SemaphoreType.DMA((STEPS - 1, HALVES, TILES, 2)),
         ],

time: 78 us -> 72 us (0.923)
  the two profiles are of different devices: /device:TPU:9 before, /device:TPU:24 now
where the time goes in v3:
time: 72 us; the launch traced here: 71.8 us
  Pallas kernels  68.6 us (95%)
  local copies, waits for them, and re-layouts  1.87 us (3%)
  between operations  1.3 us (2%)
    pallas_call x1, Pallas kernels, per_device(): pl.pallas_call(functools.partial(kernel, grid_rows, grid_cols), out_shape...  68.6 us
    unnamed x1, local copies, waits for them, and re-layouts  1.87 us

profile of v3, /device:TPU:24, one launch (start us, length us, event | category | flops | bytes accessed | tf_op | source)
XLA Modules:
  0.0 71.8 jit_solution(954725847314918508)
XLA Ops:
  1.3 68.6 %shard_map.82 = bf16[1024,256]{1,0:T(8,128)(2,1)} custom-call(s32[1,80]{1,0:T(1,128)} %bitcast.8, s32[1,80]{1,0:T(1,128)} %bitcast.9, s32[1,1]{1,0:T(1,128)S(6)} %copy.10.a_count, s32[1,20]{1,0:T(1,128)} %bitcast.10, s32[1,20]{1,0:T(1,128)} %bitcast.11, s32[1,1]{1,0:T(1,128)S(6)} %copy.11.b_count, bf16[80,128,128]{2,1,0:T(8,128)(2,1)} %bitcast.6, ...), custom_call_target="tpu_custom_call" | custom-call | tf_op jit(solution)/shard_map/pallas_call | solution.py:446
  69.9 1.9 %copy.12 = bf16[1024,256]{1,0:T(8,128)(2,1)} copy(bf16[1024,256]{1,0:T(8,128)(2,1)} %shard_map.82) | data formatting | bytes 1048576

commit v4 on v3

--- a/solution.py
+++ b/solution.py
@@ -168,9 +168,9 @@
 
     def hop_beside(s):
         return pltpu.make_async_remote_copy(
-            src_ref=b_held[s][0].at[pl.ds(0, pad_b)],
+            src_ref=b_held[s][1].at[pl.ds(0, pad_b)],
             dst_ref=passed.at[s],
-            send_sem=b_send.at[s, 0],
+            send_sem=b_send.at[s, 1],
             recv_sem=pass_recv.at[s],
             device_id=beside,
             device_id_type=MESH,
@@ -179,15 +179,15 @@
     def pass_on(s):
         return pltpu.make_async_remote_copy(
             src_ref=passed.at[s],
-            dst_ref=b_held[s + 1][0].at[pl.ds(0, pad_b)],
+            dst_ref=b_held[s + 1][1].at[pl.ds(0, pad_b)],
             send_sem=pass_send.at[s],
-            recv_sem=b_recv.at[s, 0],
+            recv_sem=b_recv.at[s, 1],
             device_id=past_beside,
             device_id_type=MESH,
         )
 
     def start_half(s, h):
-        if h > 0:
+        if h < HALVES - 1:
             half_hop(s, h).start()
             return
 
@@ -295,13 +295,14 @@
 
     loads[0].wait()
 
-    def turn(p, carry):
-        turned = b_raw[p].T
-        for h in range(HALVES):
-            b_held[0][h][p] = turned[h * strip : (h + 1) * strip, :]
-        return carry
-
-    lax.fori_loop(0, pad_b, turn, 0, unroll=True)
+    def turn(h):
+        def turn_block(p, carry):
+            b_held[0][h][p] = b_raw[p, :, h * strip : (h + 1) * strip].T
+            return carry
+
+        lax.fori_loop(0, pad_b, turn_block, 0, unroll=True)
+
+    turn(0)
     loads[1].wait()
     loads[2].wait()
     codes[0] = jnp.full((8, 128), -1, jnp.int32)
@@ -309,7 +310,9 @@
 
     pl.semaphore_wait(barrier, STEPS + jnp.where(at_first, 2, 0) + jnp.where(last_y, 1, 0))
     code_hop(0).start()
-    for h in range(HALVES):
+    start_half(0, 0)
+    for h in range(1, HALVES):
+        turn(h)
         start_half(0, h)
 
     loads[3].wait()
@@ -396,8 +399,8 @@
                 start_half(s, h)
             place_b(s, h)
             lax.fori_loop(0, TILES, functools.partial(sent_tile, s, h), 0)
-            if s < STEPS - 1 and h == 0:
-                start_pass(s)
+            if s > 1 and h == 0:
+                start_pass(s - 1)
             if s == STEPS - 1:
                 pass_home(h)
 
@@ -445,7 +448,7 @@
     strip, wide = bs // HALVES, columns // HALVES
     return pl.pallas_call(
         functools.partial(kernel, grid_rows, grid_cols),
-        out_shape=jax.ShapeDtypeStruct((rows, columns), jnp.bfloat16),
+        out_shape=pltpu.VMEM((rows, columns), jnp.bfloat16),
         in_specs=[whole, whole, smem, whole, whole, smem, whole, whole],
         out_specs=vmem,
         scratch_shapes=[

time: 72 us -> 67.2 us (0.933)
  the two profiles are of different devices: /device:TPU:24 before, /device:TPU:488 now
where the time goes in v4:
time: 67.2 us; the launch traced here: 67 us
  Pallas kernels  64.9 us (97%)
  between operations  1.3 us (2%)
  local copies, waits for them, and re-layouts  0.8 us (1%)
    pallas_call x1, Pallas kernels, per_device(): pl.pallas_call(functools.partial(kernel, grid_rows, grid_cols), out_shape...  64.9 us

profile of v4, /device:TPU:488, one launch (start us, length us, event | category | flops | bytes accessed | tf_op | source)
XLA Modules:
  0.0 67.0 jit_solution(17501365340245021060)
XLA Ops:
  1.3 64.9 %shard_map.82 = bf16[1024,256]{1,0:T(8,128)(2,1)S(1)} custom-call(s32[1,80]{1,0:T(1,128)} %bitcast.8, s32[1,80]{1,0:T(1,128)} %bitcast.9, s32[1,1]{1,0:T(1,128)S(6)} %copy.11.a_count, s32[1,20]{1,0:T(1,128)} %bitcast.10, s32[1,20]{1,0:T(1,128)} %bitcast.11, s32[1,1]{1,0:T(1,128)S(6)} %copy.12.b_count, bf16[80,128,128]{2,1,0:T(8,128)(2,1)} %bitcast.6, ...), custom_call_target="tpu_custom_call" | custom-call | tf_op jit(solution)/shard_map/pallas_call | solution.py:449
  66.2 0.8 %copy.10 = bf16[1024,256]{1,0:T(8,128)(2,1)} copy(bf16[1024,256]{1,0:T(8,128)(2,1)S(1)} %shard_map.82) | data formatting | bytes 1048576

commit v5 on v4

--- a/solution.py
+++ b/solution.py
@@ -11,8 +11,10 @@
 KB = 16
 CB = 2
 STEPS = 4
+STRIPS = 4
 HALVES = 2
 TILES = 2
+PER = STRIPS // HALVES
 
 MESH = pl.DeviceIdType.MESH
 
@@ -20,7 +22,7 @@
 def slot_codes(rows_ref, cols_ref, count_ref, block_cols):
     slots = lax.broadcasted_iota(jnp.int32, rows_ref.shape, 1)
     codes = rows_ref[...] * block_cols + cols_ref[...]
-    return jnp.where(slots < count_ref[0, 0], codes, -1)
+    return jnp.where(slots < count_ref[...], codes, -1)
 
 
 def slot_of_block(codes, blocks, empty):
@@ -36,28 +38,23 @@
     grid_cols,
     a_rows_hbm,
     a_cols_hbm,
-    a_count,
+    a_count_hbm,
     b_rows_hbm,
     b_cols_hbm,
-    b_count,
+    b_count_hbm,
     a_blocks,
     b_blocks,
     out_ref,
     a_rows,
     a_cols,
+    a_count,
     b_rows,
     b_cols,
+    b_count,
     a_held,
     a_dense,
     b_raw,
-    own_0,
-    own_1,
-    one_0,
-    one_1,
-    two_0,
-    two_1,
-    three_0,
-    three_1,
+    b_held,
     b_dense,
     codes,
     found_a,
@@ -82,12 +79,18 @@
     term_recv,
     t_send,
     t_recv,
+    last_out,
+    last_in,
+    last_scale_out,
+    last_scale_in,
+    last_send,
+    last_recv,
+    order,
 ):
     pad_a, bs = a_blocks.shape[0], a_blocks.shape[1]
     pad_b = b_blocks.shape[0]
-    strip = bs // HALVES
+    strip = bs // STRIPS
     tile = RB * bs // TILES
-    b_held = ((own_0, own_1), (one_0, one_1), (two_0, two_1), (three_0, three_1))
     i, k = lax.axis_index("row"), lax.axis_index("col")
 
     def at_col(distance):
@@ -99,7 +102,8 @@
     run, lane = grid_rows // 2, grid_cols // 2
 
     def passing(row, col):
-        return jnp.logical_and(lax.rem(row, run) == 0, lax.rem(col, lane) < lane - 2)
+        at_y = lax.rem(col, lane)
+        return jnp.logical_and(lax.rem(row, run) == 0, jnp.logical_and(at_y > 0, at_y < lane - 2))
 
     beside = (lax.rem(i + run, grid_rows), k)
     past_beside = (lax.rem(i + run + grid_rows - 1, grid_rows), lax.rem(k + 1, grid_cols))
@@ -108,8 +112,8 @@
 
     nothing = jnp.zeros((strip, bs), jnp.bfloat16)
     for held in b_held:
-        for h in range(HALVES):
-            held[h][pad_b] = nothing
+        for q in range(STRIPS):
+            held[q][pad_b] = nothing
     a_held[pad_a] = jnp.zeros((bs, bs), jnp.bfloat16)
 
     barrier = pltpu.get_barrier_semaphore()
@@ -137,8 +141,10 @@
                 (b_blocks, b_raw),
                 (b_rows_hbm, b_rows),
                 (b_cols_hbm, b_cols),
+                (b_count_hbm, b_count),
                 (a_rows_hbm, a_rows),
                 (a_cols_hbm, a_cols),
+                (a_count_hbm, a_count),
                 (a_blocks, a_held.at[pl.ds(0, pad_a)]),
             )
         )
@@ -150,60 +156,80 @@
         return pltpu.make_async_remote_copy(
             src_ref=codes.at[s],
             dst_ref=codes.at[s + 1],
-            send_sem=b_send.at[s, HALVES],
-            recv_sem=b_recv.at[s, HALVES],
+            send_sem=b_send.at[s, STRIPS],
+            recv_sem=b_recv.at[s, STRIPS],
             device_id=onward,
             device_id_type=MESH,
         )
 
-    def half_hop(s, h):
+    def strip_hop(s, q):
         return pltpu.make_async_remote_copy(
-            src_ref=b_held[s][h].at[pl.ds(0, pad_b)],
-            dst_ref=b_held[s + 1][h].at[pl.ds(0, pad_b)],
-            send_sem=b_send.at[s, h],
-            recv_sem=b_recv.at[s, h],
+            src_ref=b_held[s][q].at[pl.ds(0, pad_b)],
+            dst_ref=b_held[s + 1][q].at[pl.ds(0, pad_b)],
+            send_sem=b_send.at[s, q],
+            recv_sem=b_recv.at[s, q],
             device_id=onward,
             device_id_type=MESH,
         )
 
-    def hop_beside(s):
+    def hop_beside(s, n):
         return pltpu.make_async_remote_copy(
-            src_ref=b_held[s][1].at[pl.ds(0, pad_b)],
-            dst_ref=passed.at[s],
-            send_sem=b_send.at[s, 1],
-            recv_sem=pass_recv.at[s],
+            src_ref=b_held[s][STRIPS - PER + n].at[pl.ds(0, pad_b)],
+            dst_ref=passed.at[s, n],
+            send_sem=b_send.at[s, STRIPS - PER + n],
+            recv_sem=pass_recv.at[s, n],
             device_id=beside,
             device_id_type=MESH,
         )
 
-    def pass_on(s):
+    def pass_on(s, n):
         return pltpu.make_async_remote_copy(
-            src_ref=passed.at[s],
-            dst_ref=b_held[s + 1][1].at[pl.ds(0, pad_b)],
-            send_sem=pass_send.at[s],
-            recv_sem=b_recv.at[s, 1],
+            src_ref=passed.at[s, n],
+            dst_ref=b_held[s + 1][STRIPS - PER + n].at[pl.ds(0, pad_b)],
+            send_sem=pass_send.at[s, n],
+            recv_sem=b_recv.at[s, STRIPS - PER + n],
             device_id=past_beside,
             device_id_type=MESH,
         )
 
-    def start_half(s, h):
-        if h < HALVES - 1:
-            half_hop(s, h).start()
+    def start_strip(s, q):
+        if q < STRIPS - PER:
+            strip_hop(s, q).start()
             return
 
         @pl.when(at_first)
         def _():
-            hop_beside(s).start()
+            hop_beside(s, q - STRIPS + PER).start()
 
         @pl.when(jnp.logical_not(at_first))
         def _():
-            half_hop(s, h).start()
-
-    def start_pass(s):
+            strip_hop(s, q).start()
+
+    def start_pass(s, n):
         @pl.when(at_first)
         def _():
-            hop_beside(s).wait_recv()
-            pass_on(s).start()
+            hop_beside(s, n).wait_recv()
+            pass_on(s, n).start()
+
+    def last_home(q):
+        return (
+            pltpu.make_async_remote_copy(
+                src_ref=last_out.at[q],
+                dst_ref=last_in.at[q],
+                send_sem=last_send.at[q, 0],
+                recv_sem=last_recv.at[q, 0],
+                device_id=at_col(1 - STEPS),
+                device_id_type=MESH,
+            ),
+            pltpu.make_async_remote_copy(
+                src_ref=last_scale_out.at[q],
+                dst_ref=last_scale_in.at[q],
+                send_sem=last_send.at[q, 1],
+                recv_sem=last_recv.at[q, 1],
+                device_id=at_col(1 - STEPS),
+                device_id_type=MESH,
+            ),
+        )
 
     def tile_rows(t):
         return pl.ds(pl.multiple_of(t * tile, tile), tile)
@@ -295,28 +321,34 @@
 
     loads[0].wait()
 
-    def turn(h):
+    def turn(q):
         def turn_block(p, carry):
-            b_held[0][h][p] = b_raw[p, :, h * strip : (h + 1) * strip].T
+            b_held[0][q][p] = b_raw[p, :, q * strip : (q + 1) * strip].T
             return carry
 
         lax.fori_loop(0, pad_b, turn_block, 0, unroll=True)
 
     turn(0)
-    loads[1].wait()
-    loads[2].wait()
+    for load in loads[1:4]:
+        load.wait()
     codes[0] = jnp.full((8, 128), -1, jnp.int32)
     codes[0, 0:1, 0:pad_b] = slot_codes(b_rows, b_cols, b_count, CB)
 
     pl.semaphore_wait(barrier, STEPS + jnp.where(at_first, 2, 0) + jnp.where(last_y, 1, 0))
     code_hop(0).start()
-    start_half(0, 0)
-    for h in range(1, HALVES):
-        turn(h)
-        start_half(0, h)
-
-    loads[3].wait()
-    loads[4].wait()
+    start_strip(0, 0)
+    for q in range(1, STRIPS):
+        turn(q)
+        start_strip(0, q)
+
+    stands = lax.broadcasted_iota(jnp.int32, order.shape, 0)
+    belongs = lax.broadcasted_iota(jnp.int32, order.shape, 1)
+    strip_of, rest = stands // (CB * strip), stands % (CB * strip)
+    goes = rest // strip * bs + strip_of * strip + rest % strip
+    order[...] = jnp.where(belongs == goes, 1.0, 0.0).astype(jnp.bfloat16)
+
+    for load in loads[4:7]:
+        load.wait()
     found_a[...] = slot_of_block(slot_codes(a_rows, a_cols, a_count, KB), RB * KB, pad_a)
     a_table = pltpu.make_async_copy(found_a, where_a, table_sem.at[STEPS])
     a_table.start()
@@ -330,7 +362,7 @@
 
     find_b(0)
     a_table.wait()
-    loads[5].wait()
+    loads[7].wait()
 
     def place_a(p, carry):
         r, c = p // KB, p % KB
@@ -341,12 +373,15 @@
 
     lax.fori_loop(0, RB * KB, place_a, 0, unroll=8)
 
-    def place_b(s, h):
+    def place_b(s, strips):
         def place(r, carry):
             for c in range(CB):
-                b_dense[
-                    h, c * strip : (c + 1) * strip, pl.ds(pl.multiple_of(r * bs, bs), bs)
-                ] = b_held[s][h][where_b[s, r * CB + c, 0]]
+                slot = where_b[s, r * CB + c, 0]
+                for q in strips:
+                    first = (q % PER * CB + c) * strip
+                    b_dense[
+                        q // PER, first : first + strip, pl.ds(pl.multiple_of(r * bs, bs), bs)
+                    ] = b_held[s][q][slot]
             return carry
 
         lax.fori_loop(0, KB, place, 0, unroll=4)
@@ -359,16 +394,45 @@
             preferred_element_type=jnp.float32,
         )
 
+    def coded(term):
+        largest = jnp.maximum(jnp.max(jnp.abs(term), axis=0, keepdims=True), 1e-30)
+        code = jnp.round(term * (32767.0 / largest)).astype(jnp.int32).astype(jnp.int16)
+        return code, largest * (1.0 / 32767.0)
+
+    def send_last(q):
+        first = q % PER * CB * strip
+        parts = [
+            lax.dot_general(
+                a_dense[t * tile : (t + 1) * tile, :],
+                b_dense[q // PER, first : first + CB * strip, :],
+                (((1,), (1,)), ((), ())),
+                preferred_element_type=jnp.float32,
+            )
+            for t in range(TILES)
+        ]
+        last_out[q], last_scale_out[q] = coded(jnp.concatenate(parts, axis=1))
+        for copy in last_home(q):
+            copy.start()
+
+    def last_terms(h):
+        terms = []
+        for q in range(h * PER, (h + 1) * PER):
+            for copy in last_home(q):
+                copy.wait_recv()
+            terms.append(last_in[q].astype(jnp.float32) * last_scale_in[q])
+        wide = CB * strip
+        return [
+            jnp.concatenate([term[:, t * wide : (t + 1) * wide] for term in terms], axis=1)
+            for t in range(TILES)
+        ]
+
     def own_tile(h, t, carry):
         total[h, tile_rows(t), :] = product(h, t)
         return carry
 
     def sent_tile(s, h, t, carry):
         term = product(h, t)
-        largest = jnp.maximum(jnp.max(jnp.abs(term), axis=0, keepdims=True), 1e-30)
-        scale_out[s - 1, h, t] = largest * (1.0 / 32767.0)
-        coded = jnp.round(term * (32767.0 / largest))
-        t_out[s - 1, h, tile_rows(t), :] = coded.astype(jnp.int32).astype(jnp.int16)
+        t_out[s - 1, h, tile_rows(t), :], scale_out[s - 1, h, t] = coded(term)
         start_home(s, h, t)
         return carry
 
@@ -381,45 +445,57 @@
         total[h, tile_rows(t), :] = total[h, tile_rows(t), :] + term_from(s, h, t)
         return carry
 
+    def strips_of(h):
+        return range(h * PER, (h + 1) * PER)
+
     b_table(0).wait()
     for h in range(HALVES):
-        place_b(0, h)
+        place_b(0, strips_of(h))
         lax.fori_loop(0, TILES, functools.partial(own_tile, h), 0)
 
-    start_pass(0)
     for s in range(1, STEPS):
         code_hop(s - 1).wait_recv()
         if s < STEPS - 1:
             code_hop(s).start()
         find_b(s)
         b_table(s).wait()
-        for h in range(HALVES):
-            half_hop(s - 1, h).wait_recv()
-            if s < STEPS - 1:
-                start_half(s, h)
-            place_b(s, h)
-            lax.fori_loop(0, TILES, functools.partial(sent_tile, s, h), 0)
-            if s > 1 and h == 0:
-                start_pass(s - 1)
+        for q in range(STRIPS):
+            if q < PER:
+                start_pass(s - 1, q)
+            strip_hop(s - 1, q).wait_recv()
+            if s == STEPS - 1:
+                place_b(s, [q])
+                send_last(q)
+            else:
+                start_strip(s, q)
+            h = q // PER
+            if q % PER < PER - 1:
+                continue
             if s == STEPS - 1:
                 pass_home(h)
-
-    for s in range(1, STEPS):
+            else:
+                place_b(s, strips_of(h))
+                lax.fori_loop(0, TILES, functools.partial(sent_tile, s, h), 0)
+
+    for s in range(1, STEPS - 1):
         for h in range(HALVES):
             lax.fori_loop(0, TILES, functools.partial(add_tile, s, h), 0)
 
-    def finish(t, carry):
-        for c in range(CB):
-            strips = [total[h, tile_rows(t), c * strip : (c + 1) * strip] for h in range(HALVES)]
-            out_ref[tile_rows(t), c * bs : (c + 1) * bs] = jnp.concatenate(strips, axis=1).astype(jnp.bfloat16)
-        return carry
-
-    lax.fori_loop(0, TILES, finish, 0)
+    for h in range(HALVES - 1):
+        for t, term in enumerate(last_terms(h)):
+            total[h, t * tile : (t + 1) * tile, :] = total[h, t * tile : (t + 1) * tile, :] + term
+
+    for t, term in enumerate(last_terms(HALVES - 1)):
+        rows = slice(t * tile, (t + 1) * tile)
+        whole = [total[h, rows, :] for h in range(HALVES - 1)] + [total[HALVES - 1, rows, :] + term]
+        whole = jnp.concatenate([half.astype(jnp.bfloat16) for half in whole], axis=1)
+        out_ref[rows, :] = jnp.dot(whole, order[...], preferred_element_type=jnp.float32).astype(jnp.bfloat16)
 
     @pl.when(at_first)
     def _():
         for s in range(STEPS - 1):
-            pass_on(s).wait_send()
+            for n in range(PER):
+                pass_on(s, n).wait_send()
 
     @pl.when(last_y)
     def _():
@@ -430,11 +506,16 @@
 
     for s in range(STEPS - 1):
         code_hop(s).wait_send()
+        for q in range(STRIPS):
+            strip_hop(s, q).wait_send()
+    for s in range(1, STEPS - 1):
         for h in range(HALVES):
-            half_hop(s, h).wait_send()
             for t in range(TILES):
-                tile_home(s + 1, h, t).wait_send()
-                scale_home(s + 1, h, t).wait_send()
+                tile_home(s, h, t).wait_send()
+                scale_home(s, h, t).wait_send()
+    for q in range(STRIPS):
+        for copy in last_home(q):
+            copy.wait_send()
 
 
 def per_device(a_blocks, a_rows, a_cols, a_count, b_blocks, b_rows, b_cols, b_count):
@@ -442,24 +523,25 @@
     pad_a, bs = a_blocks.shape[2], a_blocks.shape[3]
     pad_b = b_blocks.shape[2]
     vmem = pl.BlockSpec(memory_space=pltpu.VMEM)
-    smem = pl.BlockSpec(memory_space=pltpu.SMEM)
     whole = pl.BlockSpec(memory_space=pltpu.HBM)
     rows, depth, columns = RB * bs, KB * bs, CB * bs
-    strip, wide = bs // HALVES, columns // HALVES
+    strip, wide = bs // STRIPS, columns // HALVES
     return pl.pallas_call(
         functools.partial(kernel, grid_rows, grid_cols),
         out_shape=pltpu.VMEM((rows, columns), jnp.bfloat16),
-        in_specs=[whole, whole, smem, whole, whole, smem, whole, whole],
+        in_specs=[whole] * 8,
         out_specs=vmem,
         scratch_shapes=[
             pltpu.VMEM((1, pad_a), jnp.int32),
             pltpu.VMEM((1, pad_a), jnp.int32),
+            pltpu.VMEM((1, 1), jnp.int32),
             pltpu.VMEM((1, pad_b), jnp.int32),
             pltpu.VMEM((1, pad_b), jnp.int32),
+            pltpu.VMEM((1, 1), jnp.int32),
             pltpu.VMEM((pad_a + 1, bs, bs), jnp.bfloat16),
             pltpu.VMEM((rows, depth), jnp.bfloat16),
             pltpu.VMEM((pad_b, bs, bs), jnp.bfloat16),
-            *[pltpu.VMEM((pad_b + 1, strip, bs), jnp.bfloat16)] * (STEPS * HALVES),
+            [[pltpu.VMEM((pad_b + 1, strip, bs), jnp.bfloat16)] * STRIPS] * STEPS,
             pltpu.VMEM((HALVES, wide, depth), jnp.bfloat16),
             pltpu.VMEM((STEPS, 8, 128), jnp.int32),
             pltpu.VMEM((RB * KB, 128), jnp.int32),
@@ -467,23 +549,30 @@
             pltpu.SMEM((RB * KB, 128), jnp.int32),
             pltpu.SMEM((STEPS, KB * CB, 128), jnp.int32),
             pltpu.VMEM((HALVES, rows, wide), jnp.float32),
-            pltpu.VMEM((STEPS - 1, HALVES, rows, wide), jnp.int16),
-            pltpu.VMEM((STEPS - 1, HALVES, rows, wide), jnp.int16),
-            pltpu.VMEM((STEPS - 1, HALVES, TILES, 1, wide), jnp.float32),
-            pltpu.VMEM((STEPS - 1, HALVES, TILES, 1, wide), jnp.float32),
-            pltpu.VMEM((STEPS - 1, pad_b, strip, bs), jnp.bfloat16),
-            pltpu.SemaphoreType.DMA((6,)),
+            pltpu.VMEM((STEPS - 2, HALVES, rows, wide), jnp.int16),
+            pltpu.VMEM((STEPS - 2, HALVES, rows, wide), jnp.int16),
+            pltpu.VMEM((STEPS - 2, HALVES, TILES, 1, wide), jnp.float32),
+            pltpu.VMEM((STEPS - 2, HALVES, TILES, 1, wide), jnp.float32),
+            pltpu.VMEM((STEPS - 1, PER, pad_b, strip, bs), jnp.bfloat16),
+            pltpu.SemaphoreType.DMA((8,)),
             pltpu.SemaphoreType.DMA((STEPS + 1,)),
-            pltpu.SemaphoreType.DMA((STEPS - 1, HALVES + 1)),
-            pltpu.SemaphoreType.DMA((STEPS - 1, HALVES + 1)),
-            pltpu.SemaphoreType.DMA((STEPS - 1,)),
-            pltpu.SemaphoreType.DMA((STEPS - 1,)),
+            pltpu.SemaphoreType.DMA((STEPS - 1, STRIPS + 1)),
+            pltpu.SemaphoreType.DMA((STEPS - 1, STRIPS + 1)),
+            pltpu.SemaphoreType.DMA((STEPS - 1, PER)),
+            pltpu.SemaphoreType.DMA((STEPS - 1, PER)),
             pltpu.VMEM((HALVES, rows, wide), jnp.int16),
             pltpu.VMEM((HALVES, TILES, 1, wide), jnp.float32),
             pltpu.SemaphoreType.DMA((HALVES, TILES, 2)),
             pltpu.SemaphoreType.DMA((HALVES, TILES, 2)),
-            pltpu.SemaphoreType.DMA((STEPS - 1, HALVES, TILES, 2)),
-            pltpu.SemaphoreType.DMA((STEPS - 1, HALVES, TILES, 2)),
+            pltpu.SemaphoreType.DMA((STEPS - 2, HALVES, TILES, 2)),
+            pltpu.SemaphoreType.DMA((STEPS - 2, HALVES, TILES, 2)),
+            pltpu.VMEM((STRIPS, rows // TILES, TILES * CB * strip), jnp.int16),
+            pltpu.VMEM((STRIPS, rows // TILES, TILES * CB * strip), jnp.int16),
+            pltpu.VMEM((STRIPS, 1, TILES * CB * strip), jnp.float32),
+            pltpu.VMEM((STRIPS, 1, TILES * CB * strip), jnp.float32),
+            pltpu.SemaphoreType.DMA((STRIPS, 2)),
+            pltpu.SemaphoreType.DMA((STRIPS, 2)),
+            pltpu.VMEM((columns, columns), jnp.bfloat16),
         ],
         compiler_params=pltpu.CompilerParams(
             collective_id=0, has_side_effects=True, vmem_limit_bytes=60 * 1024 * 1024

time: 67.2 us -> 65.8 us (0.979)
  the two profiles are of different devices: /device:TPU:488 before, /device:TPU:24 now
where the time goes in v5:
time: 65.8 us; the launch traced here: 64.7 us
  Pallas kernels  62.6 us (95%)
  between operations  1.3 us (2%)
  local copies, waits for them, and re-layouts  0.8 us (1%)
    pallas_call x1, Pallas kernels, per_device(): pl.pallas_call(functools.partial(kernel, grid_rows, grid_cols), out_shape...  62.6 us

profile of v5, /device:TPU:24, one launch (start us, length us, event | category | flops | bytes accessed | tf_op | source)
XLA Modules:
  0.0 64.7 jit_solution(15227011525772836491)
XLA Ops:
  1.3 62.6 %shard_map.82 = bf16[1024,256]{1,0:T(8,128)(2,1)S(1)} custom-call(s32[1,80]{1,0:T(1,128)} %bitcast.8, s32[1,80]{1,0:T(1,128)} %bitcast.9, s32[1,1]{1,0:T(1,128)S(6)} %copy.11.a_count_hbm, s32[1,20]{1,0:T(1,128)} %bitcast.10, s32[1,20]{1,0:T(1,128)} %bitcast.11, s32[1,1]{1,0:T(1,128)S(6)} %copy.12.b_count_hbm, bf16[80,128,128]{2,1,0:T(8,128)(2,1)} %bitcast.6, ...), custom_call_target="tpu_custom_call" | custom-call | tf_op jit(solution)/shard_map/pallas_call | solution.py:529
  63.9 0.8 %copy.10 = bf16[1024,256]{1,0:T(8,128)(2,1)} copy(bf16[1024,256]{1,0:T(8,128)(2,1)S(1)} %shard_map.82) | data formatting | bytes 1048576
